TPU v7x, 256 devices: a whole 4x4x8 slice. The times are simulated.
256 devices in a mesh: field: 2 (over core), sx: 8 (over y, x_lo), sy: 16 (over x_hi, z).
Axes of the slice: x: 4 (x_hi: 2, x_lo: 2; x = x_hi * 2 + x_lo), y: 4, z: 8, core: 2. Of those that a mesh axis runs over, the one named last changes fastest.
Arguments:
- inner_block: bfloat16 [4, 80, 32, 128, 128], P('field', 'sx', 'sy'), may hold values from 0.0004 to 0.03, as said below
- east_block: bfloat16 [4, 80, 32, 128, 128], P('field', 'sx', 'sy'), may hold values from 0.0004 to 0.03, as said below
- north_block: bfloat16 [4, 80, 32, 128, 128], P('field', 'sx', 'sy'), may hold values from 0.0004 to 0.03, as said below
- shift_diag: float32 [4, 80, 32, 128], P('field', 'sx', 'sy'), may hold values from 0.2 to 2
- coupling: float32 [4, 4, 80, 32, 128], P('field', None, 'sx', 'sy'), may hold values from -4 to 4
- coarse_flags: int32 [4, 80, 32, 128], P('field', 'sx', 'sy'), may hold values from 0 to 1, as said below
Outputs:
- coarse_node: bfloat16 [4, 4, 80, 32, 128, 128], P('field', None, 'sx', 'sy')
- coarse_east: bfloat16 [4, 80, 32, 128, 128], P('field', 'sx', 'sy')
- coarse_north: bfloat16 [4, 80, 32, 128, 128], P('field', 'sx', 'sy')
Inputs may be any that keep to these rules, and one draw needn't show every extreme that they name: `coarse_flags`: 1 marks a coarse point of its field; the share of coarse points is drawn for each tile and field. `inner_block`: positive magnitudes. `east_block`: positive magnitudes. `north_block`: positive magnitudes.
All inputs are finite; a program needn't handle non-finite values.
Results may differ from a plain program's by a relative error of at most 0.0046.
Values may be sent and summed in bfloat16 or wider, within the bound.
A program may use at most 128 MiB of HBM per device.

v0:
```python
import jax
import jax.numpy as jnp
from jax import lax
from jax.sharding import PartitionSpec as P


def from_behind(array, axis, by):
    devices = lax.axis_size(axis)
    pairs = [(i, i + by) for i in range(devices) if 0 <= i + by < devices]
    return lax.ppermute(array, axis, pairs)


def interpolate(matrix, shift, flags):
    tile_nodes = matrix.shape[-1]
    unit = jnp.eye(tile_nodes, dtype=bool)
    offdiag = jnp.where(unit, jnp.zeros((), matrix.dtype), matrix)
    weights = offdiag.astype(jnp.float32)
    coarse = flags.astype(jnp.float32)
    row_total = jnp.sum(weights, axis=-1)
    strong = jnp.sum(weights * coarse[..., None, :], axis=-1)
    diagonal = row_total + shift
    scaling = row_total / jnp.maximum(strong, row_total / 32.0)
    factor = (1.0 - coarse) * scaling / diagonal
    result = (
        coarse[..., :, None] * unit.astype(jnp.float32)
        + factor[..., :, None] * coarse[..., None, :] * weights
    )
    return (result.astype(jnp.bfloat16), offdiag, diagonal)


def neighbour_block(interp, coupling_block, neighbour_interp):
    image = jnp.einsum(
        "fxyik,fxykj->fxyij", coupling_block, neighbour_interp, preferred_element_type=jnp.float32
    ).astype(jnp.bfloat16)
    return (
        -jnp.einsum("fxyia,fxyib->fxyab", interp, image, preferred_element_type=jnp.float32)
    ).astype(jnp.bfloat16)


def body(inner_block, east_block, north_block, shift_diag, coupling, coarse_flags):
    field_count = inner_block.shape[0]
    interp, offdiag, diagonal = interpolate(inner_block, shift_diag, coarse_flags)
    first_field = lax.axis_index("field") * field_count
    row_fields = first_field + jnp.arange(field_count, dtype=jnp.int32)
    own_term = diagonal[..., None] * interp.astype(jnp.float32) - jnp.einsum(
        "fxyik,fxykj->fxyij", offdiag, interp, preferred_element_type=jnp.float32
    )
    column_interp = lax.all_gather(interp, "field", axis=0, tiled=True)
    members = column_interp.shape[0]
    same_field = row_fields[:, None] == jnp.arange(members, dtype=jnp.int32)[None, :]
    weighted = jnp.where(same_field[:, :, None, None, None, None], own_term[:, None], 0.0)
    weighted = (weighted + coupling[..., None] * column_interp[None].astype(jnp.float32)).astype(
        jnp.bfloat16
    )
    coarse_node = jnp.einsum(
        "fxyia,fgxyib->fgxyab", interp, weighted, preferred_element_type=jnp.float32
    ).astype(jnp.bfloat16)
    east_rim = from_behind(interp[:, :1], "sx", -1)
    north_rim = from_behind(interp[:, :, :1], "sy", -1)
    east_interp = jnp.concatenate([interp[:, 1:], east_rim], axis=1)
    north_interp = jnp.concatenate([interp[:, :, 1:], north_rim], axis=2)
    coarse_east = neighbour_block(interp, east_block, east_interp)
    coarse_north = neighbour_block(interp, north_block, north_interp)
    return (coarse_node, coarse_east, coarse_north)


def solution(mesh):
    in_specs = (
        P("field", "sx", "sy", None, None),
        P("field", "sx", "sy", None, None),
        P("field", "sx", "sy", None, None),
        P("field", "sx", "sy", None),
        P("field", None, "sx", "sy", None),
        P("field", "sx", "sy", None),
    )
    out_specs = (
        P("field", None, "sx", "sy", None, None),
        P("field", "sx", "sy", None, None),
        P("field", "sx", "sy", None, None),
    )
    return jax.shard_map(body, mesh=mesh, in_specs=in_specs, out_specs=out_specs, check_vma=False)
```

profile of v0, /device:TPU:28, one launch (start us, length us, event | category | flops | bytes accessed | tf_op | source)
XLA Modules:
  0.0 80.7 jit_solution(11037764672147897260)
XLA Ops:
  7.2 0.0 copy-start
  7.2 0.0 all-gather.2.cloned.1.call-start
  7.2 0.8 %convert_element_type.47 = f32[2,10,2,128]{3,2,1,0:T(2,128)S(1)} convert(s32[2,10,2,128]{3,2,1,0:T(2,128)} %param.11) | non-fusion elementwise | flops 5120 | bytes 40960 | tf_op jit(solution)/shard_map/convert_element_type | solution.py:18
  8.1 2.4 %fusion.6 = (f32[2,10,2,128]{3,2,1,0:T(2,128)S(1)}, f32[2,10,2,128]{3,2,1,0:T(2,128)S(1)}) fusion(f32[2,10,2,128]{3,2,1,0:T(2,128)S(1)} %convert_element_type.47, bf16[2,10,2,128,128]{4,3,2,1,0:T(8,128)(2,1)} %param.6, pred[128,128]{1,0:T(8,128)(4,1)S(1)} %get-tuple-element.15), kind=kLoop, calls=%fused_computation.11 | loop fusion | flops 3266560 | bytes 1388544 | tf_op jit(solution)/shard_map/reduce_sum | solution.py:20
  10.5 0.8 multiply_divide_fusion
  11.3 4.3 %fusion.8 = bf16[2,10,2,128,128]{4,3,2,1,0:T(8,128)(2,1)} fusion(f32[2,10,2,128]{3,2,1,0:T(2,128)S(1)} %get-tuple-element.11, f32[2,10,2,128]{3,2,1,0:T(2,128)S(1)} %convert_element_type.47, f32[128,128]{1,0:T(8,128)S(1)} %get-tuple-element.16, bf16[2,10,2,128,128]{4,3,2,1,0:T(8,128)(2,1)} %param.6, pred[128,128]{1,0:T(8,128)(4,1)S(1)} %get-tuple-element.15), kind=kLoop, calls=%fused_computation.13 | loop fusion | flops 4587520 | bytes 2744320 | tf_op jit(solution)/shard_map/convert_element_type | solution.py:28
  15.6 0.0 all-gather.2.cloned.1.call-update
  15.7 2.4 %fusion.34 = (bf16[2,10,1,128,128]{4,3,2,1,0:T(8,128)(2,1)S(1)}, bf16[2,10,1,128,128]{4,3,2,1,0:T(8,128)(2,1)}) fusion(bf16[2,10,2,128,128]{4,3,2,1,0:T(8,128)(2,1)} %fusion.8), kind=kLoop, calls=%fused_computation.37 | loop fusion | bytes 2621440 | tf_op jit(solution)/shard_map/slice | solution.py:61
  18.1 7.7 %collective-permute-start.1 = (bf16[2,10,1,128,128]{4,3,2,1,0:T(8,128)(2,1)}, bf16[2,10,1,128,128]{4,3,2,1,0:T(8,128)(2,1)}, u32[]{:S(2)}, u32[]{:S(2)}) collective-permute-start(bf16[2,10,1,128,128]{4,3,2,1,0:T(8,128)(2,1)} %get-tuple-element.14), channel_id=1, source_target_pairs={{1,0},{2,1},{3,2},{4,3},{5,4},{6,5},{7,6},{8,7},{9,8},{10,9},{11,1... | collective-permute-start | bytes 1966088 | tf_op jit(solution)/shard_map/ppermute | solution.py:10
  25.8 0.7 slice.17
  26.4 4.2 %collective-permute-start = (bf16[2,1,2,128,128]{4,3,2,1,0:T(8,128)(2,1)}, bf16[2,1,2,128,128]{4,3,2,1,0:T(8,128)(2,1)}, u32[]{:S(2)}, u32[]{:S(2)}) collective-permute-start(bf16[2,1,2,128,128]{4,3,2,1,0:T(8,128)(2,1)} %slice.17), channel_id=1, source_target_pairs={{16,0},{32,16},{48,32},{64,48},{80,64},{96,80},{112,96},{17,1},{33... | collective-permute-start | bytes 393224 | tf_op jit(solution)/shard_map/ppermute | solution.py:10
  30.6 7.0 %multiply_subtract_fusion = f32[2,10,2,128,128]{4,3,2,1,0:T(8,128)} fusion(f32[2,10,2,128]{3,2,1,0:T(2,128)S(1)} %get-tuple-element.12, bf16[2,10,2,128,128]{4,3,2,1,0:T(8,128)(2,1)} %param.6, pred[128,128]{1,0:T(8,128)(4,1)S(1)} %get-tuple-element.15, f32[2,10,2,128]{3,2,1,0:T(2,128)S(1)} %convert_element_type.47, ...), kind=kOutput, calls=%fused_computation.16 | convolution fusion | flops 179568640 | bytes 4075520 | tf_op jit(solution)/shard_map/fxyik,fxykj->fxyij/dot_general | solution.py:45
  37.6 1.1 %slice.16 = bf16[2,9,2,128,128]{4,3,2,1,0:T(8,128)(2,1)} slice(bf16[2,10,2,128,128]{4,3,2,1,0:T(8,128)(2,1)S(1)} %copy-done.1), slice={[0:2], [1:10], [0:2], [0:128], [0:128]} | slice | bytes 2359296 | tf_op jit(solution)/shard_map/slice | solution.py:60
  38.7 3.3 %copy.15 = f32[2,10,2,128,128]{3,4,2,1,0:T(8,128)} copy(f32[2,10,2,128,128]{4,3,2,1,0:T(8,128)} %multiply_subtract_fusion) | data formatting | bytes 5242880 | tf_op jit(solution)/shard_map/sub | solution.py:45
  42.0 0.9 %copy.16 = f32[2,4,10,2,128]{4,1,3,2,0:T(4,128)S(1)} copy(f32[2,4,10,2,128]{4,3,2,1,0:T(2,128)} %param.10) | data formatting | bytes 163840 | tf_op args[4]
  42.9 0.1 iota_compare_fusion.1
  43.0 0.0 collective-permute-done
  43.0 0.0 copy-done
  43.0 5.3 %negate_convert_fusion.1 = bf16[2,10,2,128,128]{4,3,2,1,0:T(8,128)(2,1)} fusion(bf16[2,10,2,128,128]{4,3,2,1,0:T(8,128)(2,1)S(1)} %copy-done, bf16[2,1,2,128,128]{4,3,2,1,0:T(8,128)(2,1)} %collective-permute-done, bf16[2,9,2,128,128]{4,3,2,1,0:T(8,128)(2,1)} %slice.16, f32[2,10,2,128]{3,2,1,0:T(2,128)S(1)} %get-tuple-element.11, ...), kind=kOutput, calls=%fused_computation.15 | convolution fusion | flops 342753280 | bytes 5365760 | tf_op jit(solution)/shard_map/fxyia,fxyib->fxyab/dot_general | solution.py:36
  48.3 0.0 collective-permute-done.1
  48.3 5.4 %negate_convert_fusion = bf16[2,10,2,128,128]{4,3,2,1,0:T(8,128)(2,1)} fusion(bf16[2,10,2,128,128]{4,3,2,1,0:T(8,128)(2,1)} %param.8, bf16[2,10,1,128,128]{4,3,2,1,0:T(8,128)(2,1)} %collective-permute-done.1, bf16[2,10,1,128,128]{4,3,2,1,0:T(8,128)(2,1)S(1)} %get-tuple-element.13, f32[2,10,2,128]{3,2,1,0:T(2,128)S(1)} %get-tuple-element.11, ...), kind=kOutput, calls=%fused_computation.14 | convolution fusion | flops 342753280 | bytes 5365760 | tf_op jit(solution)/shard_map/fxyia,fxyib->fxyab/dot_general | solution.py:36
  53.8 4.9 %copy.17 = f32[4,10,2,128,128]{3,4,0,2,1:T(8,128)} copy(bf16[4,10,2,128,128]{4,3,2,1,0:T(8,128)(2,1)} %all-gather.2.cloned.1.call-done) | data formatting | bytes 7864320 | tf_op jit(solution)/shard_map/convert_element_type | solution.py:52
  58.7 7.3 %convert_bitcast_fusion = bf16[2,4,10,2,128,128]{4,5,1,3,2,0:T(8,128)(2,1)} fusion(f32[4,10,2,128,128]{3,4,0,2,1:T(8,128)} %copy.17, f32[2,4,10,2,128]{4,1,3,2,0:T(4,128)S(1)} %copy.16, f32[2,10,2,128,128]{3,4,2,1,0:T(8,128)} %copy.15, pred[2,4]{1,0:T(4,128)(4,1)S(1)} %iota_compare_fusion.1, f32[2,10,2,128]{3,2,1,0:T(2,128)S(1)} %get-tuple-element.11, ...), kind=kOutput, calls=%fused_computation.2 | convolution fusion | flops 688783360 | bytes 14622728 | tf_op jit(solution)/shard_map/fxyia,fgxyib->fgxyab/dot_general | solution.py:55
  66.0 7.9 %copy.20 = bf16[2,4,10,2,128,128]{5,4,3,2,1,0:T(8,128)(2,1)} copy(bf16[2,4,10,2,128,128]{4,5,1,3,2,0:T(8,128)(2,1)} %convert_bitcast_fusion) | data formatting | bytes 10485760
  (7 shorter events, 0.0 us)
Async XLA Ops:
  7.2 35.9 %copy-start = (bf16[2,10,2,128,128]{4,3,2,1,0:T(8,128)(2,1)S(1)}, bf16[2,10,2,128,128]{4,3,2,1,0:T(8,128)(2,1)}, u32[]{:S(2)}) copy-start(bf16[2,10,2,128,128]{4,3,2,1,0:T(8,128)(2,1)} %param.7) | copy-start | bytes 3932164
  7.2 46.6 %all-gather.2.cloned.1.call-start = ((), (), s32[]{:S(2)}) async-start(), calls=%async_computation | async-start | bytes 3932160 | tf_op jit(solution)/shard_map/all_gather | solution.py:48
  15.6 10.1 %copy-start.1 = (bf16[2,10,2,128,128]{4,3,2,1,0:T(8,128)(2,1)S(1)}, bf16[2,10,2,128,128]{4,3,2,1,0:T(8,128)(2,1)}, u32[]{:S(2)}) copy-start(bf16[2,10,2,128,128]{4,3,2,1,0:T(8,128)(2,1)} %fusion.8) | copy-start | bytes 3932164
  18.1 30.3 %collective-permute-start.1 = (bf16[2,10,1,128,128]{4,3,2,1,0:T(8,128)(2,1)}, bf16[2,10,1,128,128]{4,3,2,1,0:T(8,128)(2,1)}, u32[]{:S(2)}, u32[]{:S(2)}) collective-permute-start(bf16[2,10,1,128,128]{4,3,2,1,0:T(8,128)(2,1)} %get-tuple-element.14), channel_id=1, source_target_pairs={{1,0},{2,1},{3,2},{4,3},{5,4},{6,5},{7,6},{8,7},{9,8},{10,9},{11,1... | collective-permute-start | bytes 1966088 | tf_op jit(solution)/shard_map/ppermute | solution.py:10
  26.4 16.6 %collective-permute-start = (bf16[2,1,2,128,128]{4,3,2,1,0:T(8,128)(2,1)}, bf16[2,1,2,128,128]{4,3,2,1,0:T(8,128)(2,1)}, u32[]{:S(2)}, u32[]{:S(2)}) collective-permute-start(bf16[2,1,2,128,128]{4,3,2,1,0:T(8,128)(2,1)} %slice.17), channel_id=1, source_target_pairs={{16,0},{32,16},{48,32},{64,48},{80,64},{96,80},{112,96},{17,1},{33... | collective-permute-start | bytes 393224 | tf_op jit(solution)/shard_map/ppermute | solution.py:10
  38.7 4.3 %copy-start.2 = (bf16[2,10,2,128,128]{4,3,2,1,0:T(8,128)(2,1)S(1)}, bf16[2,10,2,128,128]{4,3,2,1,0:T(8,128)(2,1)}, u32[]{:S(2)}) copy-start(bf16[2,10,2,128,128]{4,3,2,1,0:T(8,128)(2,1)} %param.6) | copy-start | bytes 3932164
Sparse Core Ops, SparseCore 0:
  15.8 19.3 all-gather.1
where the time goes:
time: 81.4 us; the launch traced here: 80.7 us
  matrix products  25.1 us (31%)
  local copies, waits for them, and re-layouts  21.2 us (26%)
  between operations  14.1 us (17%)
  starting transfers between devices  11.9 us (15%)
  other arithmetic  8.48 us (10%)
    ppermute x2, starting transfers between devices, from_behind(): return lax.ppermute(array, axis, pairs)  11.9 us
    dot_general x2, matrix products, neighbour_block(): jnp.einsum('fxyia,fxyib->fxyab', interp, image, preferred_element_type=jn...  10.7 us
    unnamed x8, local copies, waits for them, and re-layouts  8.83 us
    dot_general x1, matrix products, body(): jnp.einsum('fxyia,fgxyib->fgxyab', interp, weighted, preferred_element_ty...  7.32 us
    dot_general x1, matrix products, body(): jnp.einsum('fxyik,fxykj->fxyij', offdiag, interp, preferred_element_type=...  6.99 us
    convert_element_type x1, local copies, waits for them, and re-layouts, body(): column_interp[None].astype(jnp.float32)  4.89 us
    convert_element_type x1, other arithmetic, interpolate(): return (result.astype(jnp.bfloat16), offdiag, diagonal)  4.34 us
    sub x1, local copies, waits for them, and re-layouts, body(): diagonal[..., None] * interp.astype(jnp.float32)  3.31 us
  transfers between devices with their start and end apart: 3, of which 0 were waited for; matrix products, arithmetic and copies ran while one was open for 32% of the time, Pallas kernels for 0%

commit v1 on v0

v1 whole, which is shorter than its diff:
```python
import jax
import jax.numpy as jnp
from jax import lax
from jax.experimental import pallas as pl
from jax.experimental.pallas import tpu as pltpu
from jax.sharding import PartitionSpec as P

BF = jnp.bfloat16
F32 = jnp.float32
MESH = pl.DeviceIdType.MESH
NN = (((1,), (0,)), ((), ()))
NT = (((1,), (1,)), ((), ()))
MIB = 1 << 20


def mm(left, right, dims=NN):
    return lax.dot_general(left, right, dims, preferred_element_type=F32)


def iota(shape, axis):
    return lax.broadcasted_iota(jnp.int32, shape, axis)


def one_hot(dest, nodes, fine):
    row = iota((nodes, nodes), 0).astype(F32)
    place = -1.0 - dest if fine else dest
    return jnp.where(place == row, 1.0, 0.0).astype(BF)


def exchange_kernel(
    counts, inner, east, north, shift, coupling, flags,
    q_out, other_out, node_out, east_out, north_out, zn_out, ze_out, dn_out, nef_out, nec_out,
    w_v, e_v, n_v, s_v, k_v, c_v, p_v, w0_v, a_v, d_v, de_v, zns_v, zes_v, c24_v, row_v, kt_v,
    in_sem, vec_sem, en_sem, zs_sem, zr_sem, es_sem, er_sem, ds_sem, dr_sem, ps_sem, pr_sem,
):
    nsx, nsy, fields, xs, ys, m = counts
    half = m // 2
    field, sx, sy = lax.axis_index("field"), lax.axis_index("sx"), lax.axis_index("sy")
    barrier = pltpu.get_barrier_semaphore()
    partner = {"field": 1 - field}

    loads = []
    for ref, dst, k in ((flags, c_v, 0), (shift, s_v, 1), (coupling, k_v, 2)):
        copy = pltpu.make_async_copy(ref, dst, vec_sem.at[k])
        copy.start()
        loads.append(copy)

    def inner_copy(f, x):
        return pltpu.make_async_copy(inner.at[f, x], w_v.at[f, x], in_sem.at[f, x])

    for x in range(xs):
        for f in range(fields):
            inner_copy(f, x).start()

    pl.semaphore_signal(barrier, inc=1, device_id=partner, device_id_type=MESH)

    @pl.when(sy < nsy - 1)
    def _():
        pl.semaphore_signal(barrier, inc=1, device_id={"sy": sy + 1}, device_id_type=MESH)

    @pl.when(sx < nsx - 1)
    def _():
        pl.semaphore_signal(barrier, inc=1, device_id={"sx": sx + 1}, device_id_type=MESH)

    en_loads = []
    for k, (ref, dst) in enumerate(((east, e_v), (north, n_v))):
        copy = pltpu.make_async_copy(ref, dst, en_sem.at[k])
        copy.start()
        en_loads.append(copy)

    eye = iota((m, m), 0) == iota((m, m), 1)

    loads[0].wait()
    for f in range(fields):
        for x in range(xs):
            c24_v[f * xs + x : f * xs + x + 1, :] = c_v[f, x, 0:1, :].astype(F32)
        for y in range(ys):
            r = fields * xs + f * ys + y
            c24_v[r : r + 1, :] = c_v[f, 0, y : y + 1, :].astype(F32)
    rows = fields * xs + fields * ys
    c24 = c24_v[...]
    before = jnp.where(iota((m, m), 0) < iota((m, m), 1), 1.0, 0.0).astype(BF)
    rank_c = mm(c24.astype(BF), before)
    count = jnp.sum(c24, axis=1, keepdims=True)
    short = jnp.minimum(count, m - count)
    rank = jnp.where(c24 > 0.5, rank_c, iota((rows, m), 1).astype(F32) - rank_c)
    place = jnp.where(rank < half, rank, rank + short)
    d_v[...] = jnp.where(c24 > 0.5, place, -1.0 - place)

    waits = 1 + jnp.where(sy > 0, 1, 0) + jnp.where(sx > 0, 1, 0)
    pl.semaphore_wait(barrier, waits)

    def d_copy(k):
        device = {"sy": sy - 1} if k == 0 else {"sx": sx - 1}
        return pltpu.make_async_remote_copy(
            src_ref=d_v, dst_ref=(dn_out if k == 0 else de_v), send_sem=ds_sem.at[k], recv_sem=dr_sem.at[k],
            device_id=device, device_id_type=MESH)

    def zn_copy(x):
        return pltpu.make_async_remote_copy(
            src_ref=zns_v.at[x], dst_ref=zn_out.at[x], send_sem=zs_sem.at[x], recv_sem=zr_sem.at[x],
            device_id={"sy": sy - 1}, device_id_type=MESH)

    def ze_copy():
        return pltpu.make_async_remote_copy(
            src_ref=zes_v, dst_ref=ze_out, send_sem=es_sem, recv_sem=er_sem,
            device_id={"sx": sx - 1}, device_id_type=MESH)

    def p_copy(x):
        return pltpu.make_async_remote_copy(
            src_ref=p_v.at[x], dst_ref=other_out.at[x], send_sem=ps_sem.at[x], recv_sem=pr_sem.at[x],
            device_id=partner, device_id_type=MESH)

    @pl.when(sy > 0)
    def _():
        d_copy(0).start()

    @pl.when(sx > 0)
    def _():
        d_copy(1).start()

    @pl.when(sy == nsy - 1)
    def _():
        dn_out[...] = jnp.full(dn_out.shape, -1.0, F32)
        zn_out[...] = jnp.zeros(zn_out.shape, BF)

    @pl.when(sx == nsx - 1)
    def _():
        de_v[...] = jnp.full(de_v.shape, -1.0, F32)
        ze_out[...] = jnp.zeros(ze_out.shape, BF)

    loads[1].wait()

    def squeeze(p_tiles, dests):
        folded = []
        for p, dest in zip(p_tiles, dests):
            y = mm(one_hot(dest, m, True), p).astype(BF)
            x = mm(y, one_hot(dest, m, False), NT)
            beyond = x[half:, :] + pltpu.roll(x[:half, :], half, 1)
            folded.append(x[:half, :half] + beyond.T[:half, :])
        return jnp.concatenate(folded, axis=1).astype(BF)

    def interpolate(x):
        for f in range(fields):
            inner_copy(f, x).wait()
        for f in range(fields):
            for y in range(ys):
                r = f * ys + y
                row_v[r : r + 1, :] = c_v[f, x, y : y + 1, :].astype(F32)
                row_v[4 + r : 5 + r, :] = s_v[f, x, y : y + 1, :]
        vecs = row_v[...]
        cols = vecs.T
        tiles, diags = [], []
        for f in range(fields):
            for y in range(ys):
                r = f * ys + y
                c_row = vecs[r : r + 1, :]
                w0 = jnp.where(eye, 0.0, w_v[f, x, y].astype(F32))
                total = jnp.sum(w0, axis=1, keepdims=True)
                wc = w0 * c_row
                strong = jnp.sum(wc, axis=1, keepdims=True)
                diag = total + cols[:, 4 + r : 5 + r]
                alpha = total / jnp.maximum(strong, total * (1.0 / 32.0))
                factor = (1.0 - cols[:, r : r + 1]) * alpha / diag
                p = jnp.where(eye, c_row, factor * wc)
                p_b = p.astype(BF)
                p_v[x, f, y] = p_b
                q_out[x, f, y] = p.T.astype(BF)
                w0_v[x, f, y] = w0.astype(BF)
                tiles.append(p_b)
                diags.append(diag)
        a_v[x] = jnp.concatenate(diags, axis=1)
        p_copy(x).start()
        return tiles

    def send_north(x, tiles):
        dests = [d_v[pl.ds(f * xs + x, 1), :] for f in range(fields)]
        zns_v[x] = squeeze([tiles[f * ys] for f in range(fields)], dests)

        @pl.when(sy > 0)
        def _():
            zn_copy(x).start()

    first = interpolate(0)
    send_north(0, first)
    base = fields * xs
    for y in range(ys):
        dests = [d_v[base + f * ys + y : base + f * ys + y + 1, :] for f in range(fields)]
        zes_v[y] = squeeze([first[f * ys + y] for f in range(fields)], dests)

    @pl.when(sx > 0)
    def _():
        ze_copy().start()

    def phase1(x, carry):
        send_north(x, interpolate(x))
        return carry

    lax.fori_loop(1, xs, phase1, 0)

    loads[2].wait()
    for copy in en_loads:
        copy.wait()

    own0 = field * fields

    def phase2(x, carry):
        nxt = jnp.minimum(x + 1, xs - 1)
        for f in range(fields):
            for g in range(fields):
                r = (f * fields + g) * ys
                kt_v[r : r + ys, :] = k_v[f, own0 + g, x]
        kcols = kt_v[...].T
        acols = a_v[x]
        for y in range(ys):
            for f in range(fields):
                r = f * ys + y
                p = [p_v[x, g, y] for g in range(fields)]
                parts = []
                own = mm(w0_v[x, f, y], p[f])
                for g in range(fields):
                    kk = kcols[:, (f * fields + g) * ys + y : (f * fields + g) * ys + y + 1]
                    if g == f:
                        parts.append(((kk + acols[:, r : r + 1]) * p[g].astype(F32) - own).astype(BF))
                    else:
                        parts.append((kk * p[g].astype(F32)).astype(BF))
                parts.append(mm(e_v[f, x, y], p_v[nxt, f, y]).astype(BF))
                if y < ys - 1:
                    parts.append(mm(n_v[f, x, y], p_v[x, f, y + 1]).astype(BF))
                res = mm(q_out[x, f, y], jnp.concatenate(parts, axis=1))
                for g in range(fields):
                    node_out[f, g, x, y] = res[:, g * m : (g + 1) * m].astype(BF)
                east_out[f, x, y] = (-res[:, fields * m : (fields + 1) * m]).astype(BF)
                if y < ys - 1:
                    north_out[f, x, y] = (-res[:, (fields + 1) * m : (fields + 2) * m]).astype(BF)
        return carry

    lax.fori_loop(0, xs, phase2, 0)

    @pl.when(sy < nsy - 1)
    def _():
        d_copy(0).wait_recv()

    @pl.when(sx < nsx - 1)
    def _():
        d_copy(1).wait_recv()

    for y in range(ys):
        for f in range(fields):
            r = base + f * ys + y
            dn_out[r : r + 1, :] = de_v[r : r + 1, :]

    def reorder(tile, dest):
        return mm(tile, one_hot(dest, m, True), NT).astype(BF), mm(tile, one_hot(dest, m, False), NT).astype(BF)

    def phase3(x, carry):
        for f in range(fields):
            a, b = reorder(n_v[f, x, ys - 1], dn_out[pl.ds(f * xs + x, 1), :])
            nef_out[f * xs + x] = a
            nec_out[f * xs + x] = b
        return carry

    lax.fori_loop(0, xs, phase3, 0)
    for f in range(fields):
        for y in range(ys):
            r = base + f * ys + y
            a, b = reorder(e_v[f, xs - 1, y], dn_out[r : r + 1, :])
            nef_out[r] = a
            nec_out[r] = b

    def drain(x, carry):
        p_copy(x).wait()

        @pl.when(sy > 0)
        def _():
            zn_copy(x).wait_send()

        @pl.when(sy < nsy - 1)
        def _():
            zn_copy(x).wait_recv()

        return carry

    lax.fori_loop(0, xs, drain, 0)

    @pl.when(sy > 0)
    def _():
        d_copy(0).wait_send()

    @pl.when(sx > 0)
    def _():
        d_copy(1).wait_send()
        ze_copy().wait_send()

    @pl.when(sx < nsx - 1)
    def _():
        ze_copy().wait_recv()


def finish_kernel(
    counts, q, other, node_own, east_in, north_in, zn, ze, dest, nef, nec, coupling,
    node_out, east_out, north_out,
    k_v, kt_v, node_v, nrim_v, erim_v, k_sem, own_sem, int_sem, cross_sem, rim_sem,
):
    fields, xs, ys, m = counts
    half = m // 2
    field = lax.axis_index("field")
    own0, oth0 = field * fields, (1 - field) * fields
    load = pltpu.make_async_copy(coupling, k_v, k_sem)
    load.start()
    copies = []
    for f in range(fields):
        for g in range(fields):
            copies.append(pltpu.make_async_copy(node_own.at[f, g], node_out.at[f, own0 + g], own_sem.at[f, g]))
    for f in range(fields):
        copies.append(pltpu.make_async_copy(east_in.at[f, : xs - 1], east_out.at[f, : xs - 1], int_sem.at[0, f]))
        for y in range(ys - 1):
            copies.append(pltpu.make_async_copy(north_in.at[f, :, y], north_out.at[f, :, y], int_sem.at[1, f]))
    for copy in copies:
        copy.start()
    load.wait()

    def cross_copy(f, g, x):
        return pltpu.make_async_copy(node_v.at[f, g, x], node_out.at[f, oth0 + g, x], cross_sem.at[f, g, x])

    def cross(x, carry):
        for f in range(fields):
            for g in range(fields):
                r = (f * fields + g) * ys
                kt_v[r : r + ys, :] = k_v[f, oth0 + g, x]
        kcols = kt_v[...].T
        for f in range(fields):
            for y in range(ys):
                parts = []
                for g in range(fields):
                    r = (f * fields + g) * ys + y
                    parts.append((kcols[:, r : r + 1] * other[x, g, y].astype(F32)).astype(BF))
                res = mm(q[x, f, y], jnp.concatenate(parts, axis=1))
                for g in range(fields):
                    node_v[f, g, x, y] = res[:, g * m : (g + 1) * m].astype(BF)
        for f in range(fields):
            for g in range(fields):
                cross_copy(f, g, x).start()
        return carry

    lax.fori_loop(0, xs, cross, 0)

    def rim(z, k, r, d, q_tile):
        zk = z[:, k * half : (k + 1) * half]
        zt = z.T[k * half : (k + 1) * half, :]
        full = jnp.concatenate(
            [jnp.concatenate([zk, zt], axis=1), jnp.concatenate([zt, jnp.zeros_like(zt)], axis=1)], axis=0
        ).astype(BF)
        image = (mm(nef[r], full) + nec[r].astype(F32)).astype(BF)
        packed = (-mm(q_tile, image)).astype(BF)
        return mm(packed, one_hot(d, m, False)).astype(BF)

    def rim_copy(f, x):
        return pltpu.make_async_copy(nrim_v.at[f, x], north_out.at[f, x, ys - 1], rim_sem.at[f, x])

    def north_rim(x, carry):
        z = zn[x].astype(F32)
        for f in range(fields):
            r = f * xs + x
            nrim_v[f, x] = rim(z, f, r, dest[pl.ds(r, 1), :], q[x, f, ys - 1])
        for f in range(fields):
            rim_copy(f, x).start()
        return carry

    lax.fori_loop(0, xs, north_rim, 0)
    base = fields * xs
    last = []
    for y in range(ys):
        z = ze[y].astype(F32)
        for f in range(fields):
            r = base + f * ys + y
            erim_v[f, y] = rim(z, f, r, dest[r : r + 1, :], q[xs - 1, f, y])
    for f in range(fields):
        copy = pltpu.make_async_copy(erim_v.at[f], east_out.at[f, xs - 1], int_sem.at[2, f])
        copy.start()
        last.append(copy)

    def drain(x, carry):
        for f in range(fields):
            rim_copy(f, x).wait()
            for g in range(fields):
                cross_copy(f, g, x).wait()
        return carry

    lax.fori_loop(0, xs, drain, 0)
    for copy in copies + last:
        copy.wait()


def solution(mesh):
    nsx, nsy = mesh.shape["sx"], mesh.shape["sy"]

    def body(inner_block, east_block, north_block, shift_diag, coupling, coarse_flags):
        fields, xs, ys, m = inner_block.shape[:4]
        half = m // 2
        rims = fields * (xs + ys)
        every = coupling.shape[1]
        hbm = pl.BlockSpec(memory_space=pl.ANY)
        vmem = pl.BlockSpec(memory_space=pltpu.VMEM)
        dma = pltpu.SemaphoreType.DMA

        def exchange(*refs):
            exchange_kernel((nsx, nsy, fields, xs, ys, m), *refs)

        def finish(*refs):
            finish_kernel((fields, xs, ys, m), *refs)

        mid = pl.pallas_call(
            exchange,
            out_shape=[
                pltpu.VMEM((xs, fields, ys, m, m), BF),
                pltpu.VMEM((xs, fields, ys, m, m), BF),
                pltpu.VMEM((fields, fields, xs, ys, m, m), BF),
                pltpu.VMEM((fields, xs, ys, m, m), BF),
                pltpu.VMEM((fields, xs, ys, m, m), BF),
                pltpu.VMEM((xs, half, m), BF),
                pltpu.VMEM((ys, half, m), BF),
                pltpu.VMEM((rims, m), F32),
                pltpu.VMEM((rims, m, m), BF),
                pltpu.VMEM((rims, m, m), BF),
            ],
            in_specs=[hbm] * 6,
            out_specs=[vmem] * 10,
            scratch_shapes=[
                pltpu.VMEM((fields, xs, ys, m, m), BF),
                pltpu.VMEM((fields, xs, ys, m, m), BF),
                pltpu.VMEM((fields, xs, ys, m, m), BF),
                pltpu.VMEM((fields, xs, ys, m), F32),
                pltpu.VMEM((fields, every, xs, ys, m), F32),
                pltpu.VMEM((fields, xs, ys, m), jnp.int32),
                pltpu.VMEM((xs, fields, ys, m, m), BF),
                pltpu.VMEM((xs, fields, ys, m, m), BF),
                pltpu.VMEM((xs, m, fields * ys), F32),
                pltpu.VMEM((rims, m), F32),
                pltpu.VMEM((rims, m), F32),
                pltpu.VMEM((xs, half, m), BF),
                pltpu.VMEM((ys, half, m), BF),
                pltpu.VMEM((rims, m), F32),
                pltpu.VMEM((8, m), F32),
                pltpu.VMEM((8, m), F32),
                dma((fields, xs)), dma((3,)), dma((2,)),
                dma((xs,)), dma((xs,)), dma(()), dma(()), dma((2,)), dma((2,)), dma((xs,)), dma((xs,)),
            ],
            compiler_params=pltpu.CompilerParams(
                collective_id=0, has_side_effects=True, vmem_limit_bytes=24 * MIB
            ),
            name="exchange",
        )(inner_block, east_block, north_block, shift_diag, coupling, coarse_flags)

        return pl.pallas_call(
            finish,
            out_shape=[
                jax.ShapeDtypeStruct((fields, every, xs, ys, m, m), BF),
                jax.ShapeDtypeStruct((fields, xs, ys, m, m), BF),
                jax.ShapeDtypeStruct((fields, xs, ys, m, m), BF),
            ],
            in_specs=[vmem] * 10 + [hbm],
            out_specs=[hbm] * 3,
            scratch_shapes=[
                pltpu.VMEM((fields, every, xs, ys, m), F32),
                pltpu.VMEM((8, m), F32),
                pltpu.VMEM((fields, fields, xs, ys, m, m), BF),
                pltpu.VMEM((fields, xs, m, m), BF),
                pltpu.VMEM((fields, ys, m, m), BF),
                dma(()), dma((fields, fields)), dma((3, fields)), dma((fields, fields, xs)), dma((fields, xs)),
            ],
            compiler_params=pltpu.CompilerParams(vmem_limit_bytes=24 * MIB),
            name="finish",
        )(*mid, coupling)

    in_specs = (
        P("field", "sx", "sy", None, None),
        P("field", "sx", "sy", None, None),
        P("field", "sx", "sy", None, None),
        P("field", "sx", "sy", None),
        P("field", None, "sx", "sy", None),
        P("field", "sx", "sy", None),
    )
    out_specs = (
        P("field", None, "sx", "sy", None, None),
        P("field", "sx", "sy", None, None),
        P("field", "sx", "sy", None, None),
    )
    return jax.shard_map(body, mesh=mesh, in_specs=in_specs, out_specs=out_specs, check_vma=False)
```

time: 81.4 us -> 57.6 us (0.71)
  the two profiles are of different devices: /device:TPU:28 before, /device:TPU:22 now
where the time goes in v1:
time: 57.6 us; the launch traced here: 57.3 us
  Pallas kernels  50.4 us (88%)
  local copies, waits for them, and re-layouts  6.28 us (11%)
  between operations  0.65 us (1%)
    pallas_call x1, Pallas kernels, body(): pl.pallas_call(exchange, out_shape=[pltpu.VMEM((xs, fields, ys, m, m), BF...  35.5 us
    pallas_call x1, Pallas kernels, body(): pl.pallas_call(finish, out_shape=[jax.ShapeDtypeStruct((fields, every, xs...  14.9 us
    unnamed x12, local copies, waits for them, and re-layouts  6.28 us

profile of v1, /device:TPU:22, one launch (start us, length us, event | category | flops | bytes accessed | tf_op | source)
XLA Modules:
  0.0 57.3 jit_solution(1715673039477797348)
XLA Ops:
  0.6 0.0 copy-start
  0.6 1.3 %copy-done = bf16[2,10,2,128,128]{4,3,2,1,0:T(8,128)(2,1)S(1)} copy-done((bf16[2,10,2,128,128]{4,3,2,1,0:T(8,128)(2,1)S(1)}, bf16[2,10,2,128,128]{4,3,2,1,0:T(8,128)(2,1)}, u32[]{:S(2)}) %copy-start) | copy-done | bytes 1310744
  1.9 0.0 copy-start.1
  2.0 1.3 %copy-done.1 = bf16[2,10,2,128,128]{4,3,2,1,0:T(8,128)(2,1)S(1)} copy-done((bf16[2,10,2,128,128]{4,3,2,1,0:T(8,128)(2,1)S(1)}, bf16[2,10,2,128,128]{4,3,2,1,0:T(8,128)(2,1)}, u32[]{:S(2)}) %copy-start.1) | copy-done | bytes 1310744
  3.3 0.0 copy-start.2
  3.3 1.3 %copy-done.2 = bf16[2,10,2,128,128]{4,3,2,1,0:T(8,128)(2,1)S(1)} copy-done((bf16[2,10,2,128,128]{4,3,2,1,0:T(8,128)(2,1)S(1)}, bf16[2,10,2,128,128]{4,3,2,1,0:T(8,128)(2,1)}, u32[]{:S(2)}) %copy-start.2) | copy-done | bytes 1310744
  4.6 0.0 copy-start.3
  4.6 0.9 %copy-done.3 = f32[2,4,10,2,128]{4,3,2,1,0:T(2,128)S(1)} copy-done((f32[2,4,10,2,128]{4,3,2,1,0:T(2,128)S(1)}, f32[2,4,10,2,128]{4,3,2,1,0:T(2,128)}, u32[]{:S(2)}) %copy-start.3) | copy-done | bytes 81944
  5.5 0.0 copy-start.4
  5.5 0.7 %copy-done.4 = f32[2,10,2,128]{3,2,1,0:T(2,128)S(1)} copy-done((f32[2,10,2,128]{3,2,1,0:T(2,128)S(1)}, f32[2,10,2,128]{3,2,1,0:T(2,128)}, u32[]{:S(2)}) %copy-start.4) | copy-done | bytes 20504
  6.2 0.0 copy-start.5
  6.2 0.7 %copy-done.5 = s32[2,10,2,128]{3,2,1,0:T(2,128)S(1)} copy-done((s32[2,10,2,128]{3,2,1,0:T(2,128)S(1)}, s32[2,10,2,128]{3,2,1,0:T(2,128)}, u32[]{:S(2)}) %copy-start.5) | copy-done | bytes 20504
  6.9 35.5 %exchange.1 = (bf16[10,2,2,128,128]{4,3,2,1,0:T(8,128)(2,1)S(1)}, bf16[10,2,2,128,128]{4,3,2,1,0:T(8,128)(2,1)S(1)}, bf16[2,2,10,2,128,128]{5,4,3,2,1,0:T(8,128)...) custom-call(bf16[2,10,2,128,128]{4,3,2,1,0:T(8,128)(2,1)S(1)} %copy-, ...), custom_call_target="tpu_custom_call" | custom-call | tf_op jit(solution)/shard_map/exchange/pallas_call | solution.py:413
  42.4 14.9 %finish.1 = (bf16[2,4,10,2,128,128]{5,4,3,2,1,0:T(8,128)(2,1)}, bf16[2,10,2,128,128]{4,3,2,1,0:T(8,128)(2,1)}, bf16[2,10,2,128,128]{4,3,2,1,0:T(8,128)(2,1)}) custom-call(bf16[10,2,2,128,128]{4,3,2,1,0:T(8,128)(2,1)S(1)} %get-tuple-element.13.refs_0_, bf16[10,2,2,128,128]{4,3,2,1,0:T(8,128)(2,1)S(1)} %get-tuple-element.14.refs_1_, ...), custom_call_target="tpu_custom_call" | custom-call | tf_op jit(solution)/shard_map/finish/pallas_call | solution.py:455
Async XLA Ops:
  0.6 1.3 %copy-start = (bf16[2,10,2,128,128]{4,3,2,1,0:T(8,128)(2,1)S(1)}, bf16[2,10,2,128,128]{4,3,2,1,0:T(8,128)(2,1)}, u32[]{:S(2)}) copy-start(bf16[2,10,2,128,128]{4,3,2,1,0:T(8,128)(2,1)} %refs_0_.1) | copy-start | bytes 3932164
  1.9 1.3 %copy-start.1 = (bf16[2,10,2,128,128]{4,3,2,1,0:T(8,128)(2,1)S(1)}, bf16[2,10,2,128,128]{4,3,2,1,0:T(8,128)(2,1)}, u32[]{:S(2)}) copy-start(bf16[2,10,2,128,128]{4,3,2,1,0:T(8,128)(2,1)} %refs_1_.1) | copy-start | bytes 3932164
  3.3 1.3 %copy-start.2 = (bf16[2,10,2,128,128]{4,3,2,1,0:T(8,128)(2,1)S(1)}, bf16[2,10,2,128,128]{4,3,2,1,0:T(8,128)(2,1)}, u32[]{:S(2)}) copy-start(bf16[2,10,2,128,128]{4,3,2,1,0:T(8,128)(2,1)} %refs_2_.1) | copy-start | bytes 3932164
  4.6 0.9 %copy-start.3 = (f32[2,4,10,2,128]{4,3,2,1,0:T(2,128)S(1)}, f32[2,4,10,2,128]{4,3,2,1,0:T(2,128)}, u32[]{:S(2)}) copy-start(f32[2,4,10,2,128]{4,3,2,1,0:T(2,128)} %refs_10_.1) | copy-start | bytes 245764
  5.5 0.7 %copy-start.4 = (f32[2,10,2,128]{3,2,1,0:T(2,128)S(1)}, f32[2,10,2,128]{3,2,1,0:T(2,128)}, u32[]{:S(2)}) copy-start(f32[2,10,2,128]{3,2,1,0:T(2,128)} %refs_3_.1) | copy-start | bytes 61444
  6.2 0.7 %copy-start.5 = (s32[2,10,2,128]{3,2,1,0:T(2,128)S(1)}, s32[2,10,2,128]{3,2,1,0:T(2,128)}, u32[]{:S(2)}) copy-start(s32[2,10,2,128]{3,2,1,0:T(2,128)} %refs_5_.1) | copy-start | bytes 61444

commit v2 on v0

v2 whole, which is shorter than its diff:
```python
import jax
import jax.numpy as jnp
from jax import lax
from jax.experimental import pallas as pl
from jax.experimental.pallas import tpu as pltpu
from jax.sharding import PartitionSpec as P

BF = jnp.bfloat16
F32 = jnp.float32
MESH = pl.DeviceIdType.MESH
NN = (((1,), (0,)), ((), ()))
NT = (((1,), (1,)), ((), ()))
MIB = 1 << 20
PAD = 24


def mm(left, right, dims=NN):
    return lax.dot_general(left, right, dims, preferred_element_type=F32)


def iota(shape, axis):
    return lax.broadcasted_iota(jnp.int32, shape, axis)


def fine_hot(dest, m):
    return jnp.where(-1.0 - dest == iota((m, m), 0).astype(F32), 1.0, 0.0).astype(BF)


def coarse_hot(dest, m):
    return jnp.where(dest == iota((m, m), 0).astype(F32), 1.0, 0.0).astype(BF)


def exchange_kernel(
    dims, inner, east, north, shift, coupling, flags,
    q_out, other_out, node_out, east_out, north_out, zn_out, ze_out, dn_out, de_out, ne_out, kt_out,
    w_v, e_v, n_v, s_v, k_v, c_v, p_v, w0_v, wt_v, c_r, s_r, a_r, tot_r, str_r, k_r, fac_t, d_v, y_v, x_v,
    zns_v, zes_v, eye_v, off_v,
    w_sem, vec_sem, en_sem, zs_sem, zr_sem, es_sem, er_sem, ds_sem, dr_sem, ps_sem, pr_sem,
):
    nsx, nsy, fields, xs, ys, m = dims
    half = m // 2
    tiles = [(x, f) for x in range(xs) for f in range(fields)]
    field, sx, sy = lax.axis_index("field"), lax.axis_index("sx"), lax.axis_index("sy")
    barrier = pltpu.get_barrier_semaphore()
    partner = {"field": 1 - field}

    flag_load = pltpu.make_async_copy(flags, c_v, vec_sem.at[0])
    shift_load = pltpu.make_async_copy(shift, s_v, vec_sem.at[1])
    k_load = pltpu.make_async_copy(coupling, k_v, vec_sem.at[2])
    w_loads = [pltpu.make_async_copy(inner.at[:, :, y], w_v.at[y], w_sem.at[y]) for y in range(ys)]
    e_load = pltpu.make_async_copy(east, e_v, en_sem.at[0])
    n_load = pltpu.make_async_copy(north, n_v, en_sem.at[1])
    flag_load.start()
    w_loads[0].start()
    shift_load.start()
    for copy in w_loads[1:]:
        copy.start()

    pl.semaphore_signal(barrier, inc=1, device_id=partner, device_id_type=MESH)

    @pl.when(sy < nsy - 1)
    def _():
        pl.semaphore_signal(barrier, inc=1, device_id={"sy": sy + 1}, device_id_type=MESH)

    @pl.when(sx < nsx - 1)
    def _():
        pl.semaphore_signal(barrier, inc=1, device_id={"sx": sx + 1}, device_id_type=MESH)

    k_load.start()
    e_load.start()
    n_load.start()

    unit = iota((m, m), 0) == iota((m, m), 1)
    eye_v[...] = jnp.where(unit, 1.0, 0.0).astype(BF)
    off_v[...] = jnp.where(unit, 0.0, 1.0).astype(BF)

    c_r[...] = jnp.zeros(c_r.shape, F32)
    s_r[...] = jnp.ones(s_r.shape, F32)
    k_r[...] = jnp.zeros(k_r.shape, F32)
    tot_r[...] = jnp.ones(tot_r.shape, F32)
    str_r[...] = jnp.ones(str_r.shape, F32)
    flag_load.wait()
    for t, (x, f) in enumerate(tiles):
        row = c_v[f, x].astype(F32)
        for y in range(ys):
            c_r[y, t : t + 1, :] = row[y : y + 1, :]
    before = jnp.where(iota((m, m), 0) < iota((m, m), 1), 1.0, 0.0).astype(BF)
    for y in range(ys):
        c = c_r[y]
        rank_c = mm(c.astype(BF), before)
        count = jnp.sum(c, axis=1, keepdims=True)
        short = jnp.minimum(count, m - count)
        rank = jnp.where(c > 0.5, rank_c, iota((PAD, m), 1).astype(F32) - rank_c)
        place = jnp.where(rank < half, rank, rank + short)
        d_v[y] = jnp.where(c > 0.5, place, -1.0 - place)

    pl.semaphore_wait(barrier, 1 + jnp.where(sy > 0, 1, 0) + jnp.where(sx > 0, 1, 0))

    def to_north(src, dst, send, recv):
        return pltpu.make_async_remote_copy(
            src_ref=src, dst_ref=dst, send_sem=send, recv_sem=recv, device_id={"sy": sy - 1}, device_id_type=MESH)

    def to_east(src, dst, send, recv):
        return pltpu.make_async_remote_copy(
            src_ref=src, dst_ref=dst, send_sem=send, recv_sem=recv, device_id={"sx": sx - 1}, device_id_type=MESH)

    dn_copy = to_north(d_v.at[0], dn_out, ds_sem.at[0], dr_sem.at[0])
    de_copy = to_east(d_v.at[:, 0:8], de_out, ds_sem.at[1], dr_sem.at[1])
    zn_copies = [to_north(zns_v.at[x], zn_out.at[x], zs_sem.at[x], zr_sem.at[x]) for x in range(xs)]
    ze_copies = [
        to_east(zns_v.at[0] if y == 0 else zes_v.at[y], ze_out.at[y], es_sem.at[y], er_sem.at[y]) for y in range(ys)
    ]
    p_copies = [
        pltpu.make_async_remote_copy(
            src_ref=p_v.at[y], dst_ref=other_out.at[y], send_sem=ps_sem.at[y], recv_sem=pr_sem.at[y],
            device_id=partner, device_id_type=MESH)
        for y in range(ys)
    ]

    @pl.when(sy > 0)
    def _():
        dn_copy.start()

    @pl.when(sx > 0)
    def _():
        de_copy.start()

    @pl.when(sy == nsy - 1)
    def _():
        dn_out[...] = jnp.full(dn_out.shape, -1.0, F32)
        zn_out[...] = jnp.zeros(zn_out.shape, BF)

    @pl.when(sx == nsx - 1)
    def _():
        de_out[...] = jnp.full(de_out.shape, -1.0, F32)
        ze_out[...] = jnp.zeros(ze_out.shape, BF)

    shift_load.wait()
    for t, (x, f) in enumerate(tiles):
        row = s_v[f, x]
        for y in range(ys):
            s_r[y, t : t + 1, :] = row[y : y + 1, :]

    def interpolate(y):
        for x in range(xs):
            left = jnp.concatenate(
                [jnp.ones((1, m), F32), c_r[y, x * fields : (x + 1) * fields, :], jnp.zeros((15 - fields, m), F32)], axis=0
            ).astype(BF)
            for f in range(fields):
                t = x * fields + f
                w0 = w_v[y, f, x] * off_v[...]
                w0_v[y, x, f] = w0
                sums = mm(left, w0, NT)
                tot_r[y, t : t + 1, :] = sums[0:1, :]
                str_r[y, t : t + 1, :] = sums[1 + f : 2 + f, :]
        total, c = tot_r[y], c_r[y]
        diag = total + s_r[y]
        alpha = total / jnp.maximum(str_r[y], total * (1.0 / 32.0))
        factor = (1.0 - c) * alpha / diag
        a_r[y] = diag
        fac_t[y] = jnp.concatenate([factor, jnp.zeros((m - PAD, m), F32)], axis=0).T
        for t, (x, f) in enumerate(tiles):
            chosen = jnp.broadcast_to(c_r[y, t : t + 1, :], (m, m)).astype(BF)
            scaled = (fac_t[y, :, t : t + 1] * w0_v[y, x, f].astype(F32)).astype(BF)
            p_v[y, x, f] = scaled * chosen + eye_v[...] * chosen

    def squeeze(y, some):
        for x, f in some:
            t = x * fields + f
            y_v[y, t] = mm(fine_hot(d_v[y, t : t + 1, :], m), p_v[y, x, f]).astype(BF)
        for x, f in some:
            t = x * fields + f
            x_v[y, t] = mm(y_v[y, t], coarse_hot(d_v[y, t : t + 1, :], m), NT).astype(BF)

    def folded(y, x):
        parts = []
        for f in range(fields):
            t = x * fields + f
            turned = x_v[y, t].T
            parts.append(x_v[y, t, :half, :half] + turned[:half, half:] + turned[half:, :half])
        return jnp.concatenate(parts, axis=1)

    w_loads[0].wait()
    interpolate(0)
    squeeze(0, tiles)
    for x in range(xs):
        zns_v[x] = folded(0, x)

        @pl.when(sy > 0)
        def _():
            zn_copies[x].start()

    @pl.when(sx > 0)
    def _():
        ze_copies[0].start()

    p_copies[0].start()
    for y in range(1, ys):
        w_loads[y].wait()
        interpolate(y)
        squeeze(y, tiles[:fields])
        zes_v[y] = folded(y, 0)

        @pl.when(sx > 0)
        def _():
            ze_copies[y].start()

        p_copies[y].start()

    for y in range(ys):
        for x, f in tiles:
            q_out[y, x, f] = p_v[y, x, f].T

    k_load.wait()
    own0, oth0 = field * fields, (1 - field) * fields
    for t, (x, f) in enumerate(tiles):
        rows = [k_v[f, own0 + f, x], k_v[f, own0 + (1 - f), x], k_v[f, oth0, x], k_v[f, oth0 + 1, x]]
        for j, row in enumerate(rows):
            for y in range(ys):
                k_r[y, j * PAD + t : j * PAD + t + 1, :] = row[y : y + 1, :]
    for y in range(ys):
        k_r[y, :PAD, :] = k_r[y, :PAD, :] + a_r[y]
        kt_out[y] = k_r[y].T

    e_load.wait()
    n_load.wait()

    def column(j, y, t):
        return kt_out[y, :, j * PAD + t : j * PAD + t + 1]

    for y in range(ys):
        for t, (x, f) in enumerate(tiles):
            p = p_v[y, x, f]
            own = mm(w0_v[y, x, f], p)
            wt_v[y, x, f, :, f * m : (f + 1) * m] = (column(0, y, t) * p.astype(F32) - own).astype(BF)
            wt_v[y, x, f, :, (1 - f) * m : (2 - f) * m] = (column(1, y, t) * p_v[y, x, 1 - f].astype(F32)).astype(BF)
            if x < xs - 1:
                wt_v[y, x, f, :, 2 * m : 3 * m] = mm(e_v[f, x, y], p_v[y, x + 1, f]).astype(BF)
            if y < ys - 1:
                wt_v[y, x, f, :, 3 * m : 4 * m] = mm(n_v[f, x, y], p_v[y + 1, x, f]).astype(BF)
    for y in range(ys):
        for x, f in tiles:
            q = q_out[y, x, f]
            res = mm(q, wt_v[y, x, f, :, : 2 * m])
            for g in range(fields):
                node_out[f, g, x, y] = res[:, g * m : (g + 1) * m].astype(BF)
            if x < xs - 1:
                east_out[f, x, y] = (-mm(q, wt_v[y, x, f, :, 2 * m : 3 * m])).astype(BF)
            if y < ys - 1:
                north_out[f, x, y] = (-mm(q, wt_v[y, x, f, :, 3 * m : 4 * m])).astype(BF)

    @pl.when(sy < nsy - 1)
    def _():
        dn_copy.wait_recv()

    @pl.when(sx < nsx - 1)
    def _():
        de_copy.wait_recv()

    def reorder(tile, dest):
        return mm(tile, jnp.concatenate([fine_hot(dest, m), coarse_hot(dest, m)], axis=0), NT).astype(BF)

    for t, (x, f) in enumerate(tiles):
        ne_out[t] = reorder(n_v[f, x, ys - 1], dn_out[t : t + 1, :])
    for y in range(ys):
        for f in range(fields):
            ne_out[len(tiles) + y * fields + f] = reorder(e_v[f, xs - 1, y], de_out[y, f : f + 1, :])

    @pl.when(sy > 0)
    def _():
        dn_copy.wait_send()
        for copy in zn_copies:
            copy.wait_send()

    @pl.when(sx > 0)
    def _():
        de_copy.wait_send()
        for copy in ze_copies:
            copy.wait_send()

    for copy in p_copies:
        copy.wait()

    @pl.when(sx < nsx - 1)
    def _():
        for copy in ze_copies:
            copy.wait_recv()

    @pl.when(sy < nsy - 1)
    def _():
        for copy in zn_copies:
            copy.wait_recv()


def finish_kernel(
    dims, q, other, node_own, east_in, north_in, zn, ze, dn, de, ne, kt,
    node_out, east_out, north_out,
    wt_v, node_v, full_v, im_v, pk_v, nrim_v, erim_v, own_sem, int_sem, cross_sem, rim_sem,
):
    fields, xs, ys, m = dims
    half = m // 2
    tiles = [(x, f) for x in range(xs) for f in range(fields)]
    field = lax.axis_index("field")
    own0, oth0 = field * fields, (1 - field) * fields
    copies = []

    def put(src, dst, sem):
        copy = pltpu.make_async_copy(src, dst, sem)
        copy.start()
        copies.append(copy)

    for f in range(fields):
        for g in range(fields):
            put(node_own.at[f, g], node_out.at[f, own0 + g], own_sem.at[f, g])
    for f in range(fields):
        put(east_in.at[f, : xs - 1], east_out.at[f, : xs - 1], int_sem.at[0, f])
        put(north_in.at[f, :, 0], north_out.at[f, :, 0], int_sem.at[1, f])

    def column(j, y, t):
        return kt[y, :, j * PAD + t : j * PAD + t + 1]

    for y in range(ys):
        for t, (x, f) in enumerate(tiles):
            for g in range(fields):
                wt_v[y, x, f, :, g * m : (g + 1) * m] = (column(2 + g, y, t) * other[y, x, g].astype(F32)).astype(BF)
    for x in range(xs):
        for f in range(fields):
            for y in range(ys):
                res = mm(q[y, x, f], wt_v[y, x, f])
                for g in range(fields):
                    node_v[f, g, x, y] = res[:, g * m : (g + 1) * m].astype(BF)
            for g in range(fields):
                put(node_v.at[f, g, x], node_out.at[f, oth0 + g, x], cross_sem.at[f, g, x])

    rims = []
    for t, (x, f) in enumerate(tiles):
        rims.append((zn, x, f, q.at[ys - 1, x, f], dn.at[t : t + 1, :]))
    for y in range(ys):
        for f in range(fields):
            rims.append((ze, y, f, q.at[y, xs - 1, f], de.at[y, f : f + 1, :]))
    for r, (z, i, f, _, _) in enumerate(rims):
        turned = z[i].T[f * half : (f + 1) * half, :]
        full_v[r, :half, :half] = z[i, :, f * half : (f + 1) * half]
        full_v[r, half:, :half] = turned
        full_v[r, :half, half:] = turned
        full_v[r, half:, half:] = jnp.zeros((half, half), BF)
    for r in range(len(rims)):
        im_v[r] = (mm(ne[r, :, :m], full_v[r]) + ne[r, :, m:].astype(F32)).astype(BF)
    for r, (_, _, _, tile, _) in enumerate(rims):
        pk_v[r] = (-mm(tile[...], im_v[r])).astype(BF)
    for t, (x, f) in enumerate(tiles):
        nrim_v[f, x] = mm(pk_v[t], coarse_hot(rims[t][4][...], m)).astype(BF)
    for f in range(fields):
        put(nrim_v.at[f], north_out.at[f, :, ys - 1], rim_sem.at[0, f])
    for y in range(ys):
        for f in range(fields):
            r = len(tiles) + y * fields + f
            erim_v[f, y] = mm(pk_v[r], coarse_hot(rims[r][4][...], m)).astype(BF)
    for f in range(fields):
        put(erim_v.at[f], east_out.at[f, xs - 1], rim_sem.at[1, f])
    for copy in copies:
        copy.wait()


def solution(mesh):
    nsx, nsy = mesh.shape["sx"], mesh.shape["sy"]

    def body(inner_block, east_block, north_block, shift_diag, coupling, coarse_flags):
        fields, xs, ys, m = inner_block.shape[:4]
        half = m // 2
        rims = fields * (xs + ys)
        every = coupling.shape[1]
        hbm = pl.BlockSpec(memory_space=pltpu.HBM)
        vmem = pl.BlockSpec(memory_space=pltpu.VMEM)
        dma = pltpu.SemaphoreType.DMA

        def exchange(*refs):
            exchange_kernel((nsx, nsy, fields, xs, ys, m), *refs)

        def finish(*refs):
            finish_kernel((fields, xs, ys, m), *refs)

        mid = pl.pallas_call(
            exchange,
            out_shape=[
                pltpu.VMEM((ys, xs, fields, m, m), BF),
                pltpu.VMEM((ys, xs, fields, m, m), BF),
                pltpu.VMEM((fields, fields, xs, ys, m, m), BF),
                pltpu.VMEM((fields, xs, ys, m, m), BF),
                pltpu.VMEM((fields, xs, ys, m, m), BF),
                pltpu.VMEM((xs, half, m), BF),
                pltpu.VMEM((ys, half, m), BF),
                pltpu.VMEM((PAD, m), F32),
                pltpu.VMEM((ys, 8, m), F32),
                pltpu.VMEM((rims, m, 2 * m), BF),
                pltpu.VMEM((ys, m, m), F32),
            ],
            in_specs=[hbm] * 6,
            out_specs=[vmem] * 11,
            scratch_shapes=[
                pltpu.VMEM((ys, fields, xs, m, m), BF),
                pltpu.VMEM((fields, xs, ys, m, m), BF),
                pltpu.VMEM((fields, xs, ys, m, m), BF),
                pltpu.VMEM((fields, xs, ys, m), F32),
                pltpu.VMEM((fields, every, xs, ys, m), F32),
                pltpu.VMEM((fields, xs, ys, m), jnp.int32),
                pltpu.VMEM((ys, xs, fields, m, m), BF),
                pltpu.VMEM((ys, xs, fields, m, m), BF),
                pltpu.VMEM((ys, xs, fields, m, 4 * m), BF),
                pltpu.VMEM((ys, PAD, m), F32),
                pltpu.VMEM((ys, PAD, m), F32),
                pltpu.VMEM((ys, PAD, m), F32),
                pltpu.VMEM((ys, PAD, m), F32),
                pltpu.VMEM((ys, PAD, m), F32),
                pltpu.VMEM((ys, m, m), F32),
                pltpu.VMEM((ys, m, m), F32),
                pltpu.VMEM((ys, PAD, m), F32),
                pltpu.VMEM((ys, PAD, m, m), BF),
                pltpu.VMEM((ys, PAD, m, m), BF),
                pltpu.VMEM((xs, half, m), BF),
                pltpu.VMEM((ys, half, m), BF),
                pltpu.VMEM((m, m), BF),
                pltpu.VMEM((m, m), BF),
                dma((ys,)), dma((3,)), dma((2,)),
                dma((xs,)), dma((xs,)), dma((ys,)), dma((ys,)), dma((2,)), dma((2,)), dma((ys,)), dma((ys,)),
            ],
            compiler_params=pltpu.CompilerParams(
                collective_id=0, has_side_effects=True, vmem_limit_bytes=32 * MIB
            ),
            name="exchange",
        )(*[
            pltpu.with_memory_space_constraint(a, pltpu.HBM)
            for a in (inner_block, east_block, north_block, shift_diag, coupling, coarse_flags)
        ])

        return pl.pallas_call(
            finish,
            out_shape=[
                jax.ShapeDtypeStruct((fields, every, xs, ys, m, m), BF),
                jax.ShapeDtypeStruct((fields, xs, ys, m, m), BF),
                jax.ShapeDtypeStruct((fields, xs, ys, m, m), BF),
            ],
            in_specs=[vmem] * 11,
            out_specs=[hbm] * 3,
            scratch_shapes=[
                pltpu.VMEM((ys, xs, fields, m, 2 * m), BF),
                pltpu.VMEM((fields, fields, xs, ys, m, m), BF),
                pltpu.VMEM((rims, m, m), BF),
                pltpu.VMEM((rims, m, m), BF),
                pltpu.VMEM((rims, m, m), BF),
                pltpu.VMEM((fields, xs, m, m), BF),
                pltpu.VMEM((fields, ys, m, m), BF),
                dma((fields, fields)), dma((2, fields)), dma((fields, fields, xs)), dma((2, fields)),
            ],
            compiler_params=pltpu.CompilerParams(vmem_limit_bytes=24 * MIB),
            name="finish",
        )(*mid)

    in_specs = (
        P("field", "sx", "sy", None, None),
        P("field", "sx", "sy", None, None),
        P("field", "sx", "sy", None, None),
        P("field", "sx", "sy", None),
        P("field", None, "sx", "sy", None),
        P("field", "sx", "sy", None),
    )
    out_specs = (
        P("field", None, "sx", "sy", None, None),
        P("field", "sx", "sy", None, None),
        P("field", "sx", "sy", None, None),
    )
    return jax.shard_map(body, mesh=mesh, in_specs=in_specs, out_specs=out_specs, check_vma=False)
```

time: 81.4 us -> 21.4 us (0.26)
  the two profiles are of different devices: /device:TPU:28 before, /device:TPU:22 now
where the time goes in v2:
time: 21.4 us; the launch traced here: 21.3 us
  Pallas kernels  20.7 us (97%)
  between operations  0.64 us (3%)
    pallas_call x1, Pallas kernels, body(): pl.pallas_call(exchange, out_shape=[pltpu.VMEM((ys, xs, fields, m, m), BF...  16.2 us
    pallas_call x1, Pallas kernels, body(): pl.pallas_call(finish, out_shape=[jax.ShapeDtypeStruct((fields, every, xs...  4.47 us

profile of v2, /device:TPU:22, one launch (start us, length us, event | category | flops | bytes accessed | tf_op | source)
XLA Modules:
  0.0 21.3 jit_solution(1582923815030072840)
XLA Ops:
  0.6 16.2 %exchange.1 = (bf16[2,10,2,128,128]{4,3,2,1,0:T(8,128)(2,1)S(1)}, bf16[2,10,2,128,128]{4,3,2,1,0:T(8,128)(2,1)S(1)}, bf16[2,2,10,2,128,128]{5,4,3,2,1,0:T(8,128)...) custom-call(bf16[2,10,2,128,128]{4,3,2,1,0:T(8,128)(2,1)} %refs_0_.1, ...), custom_call_target="tpu_custom_call" | custom-call | tf_op jit(solution)/shard_map/exchange/pallas_call | solution.py:383
  16.8 4.5 %finish.1 = (bf16[2,4,10,2,128,128]{5,4,3,2,1,0:T(8,128)(2,1)}, bf16[2,10,2,128,128]{4,3,2,1,0:T(8,128)(2,1)}, bf16[2,10,2,128,128]{4,3,2,1,0:T(8,128)(2,1)}) custom-call(bf16[2,10,2,128,128]{4,3,2,1,0:T(8,128)(2,1)S(1)} %get-tuple-element.14.refs_0_, bf16[2,10,2,128,128]{4,3,2,1,0:T(8,128)(2,1)S(1)} %get-tuple-element.15.refs_1_, ...), custom_call_target="tpu_custom_call" | custom-call | tf_op jit(solution)/shard_map/finish/pallas_call | solution.py:436

commit v3 on v2

--- a/solution.py
+++ b/solution.py
@@ -32,14 +32,16 @@
 
 def exchange_kernel(
     dims, inner, east, north, shift, coupling, flags,
-    q_out, other_out, node_out, east_out, north_out, zn_out, ze_out, dn_out, de_out, ne_out, kt_out,
+    q_out, cross_out, node_out, east_out, north_out, zn_out, ze_out, dn_out, de_out, ne_out,
     w_v, e_v, n_v, s_v, k_v, c_v, p_v, w0_v, wt_v, c_r, s_r, a_r, tot_r, str_r, k_r, fac_t, d_v, y_v, x_v,
-    zns_v, zes_v, eye_v, off_v,
+    zns_v, zes_v, eye_v, off_v, dnr_v, der_v, other_v, wo_v, kt_v,
     w_sem, vec_sem, en_sem, zs_sem, zr_sem, es_sem, er_sem, ds_sem, dr_sem, ps_sem, pr_sem,
 ):
     nsx, nsy, fields, xs, ys, m = dims
     half = m // 2
     tiles = [(x, f) for x in range(xs) for f in range(fields)]
+    step = -(-xs // 2)
+    groups = [(a, min(a + step, xs)) for a in range(0, xs, step)]
     field, sx, sy = lax.axis_index("field"), lax.axis_index("sx"), lax.axis_index("sy")
     barrier = pltpu.get_barrier_semaphore()
     partner = {"field": 1 - field}
@@ -52,23 +54,15 @@
     n_load = pltpu.make_async_copy(north, n_v, en_sem.at[1])
     flag_load.start()
     w_loads[0].start()
-    shift_load.start()
-    for copy in w_loads[1:]:
-        copy.start()
 
     pl.semaphore_signal(barrier, inc=1, device_id=partner, device_id_type=MESH)
 
+
     @pl.when(sy < nsy - 1)
     def _():
         pl.semaphore_signal(barrier, inc=1, device_id={"sy": sy + 1}, device_id_type=MESH)
 
-    @pl.when(sx < nsx - 1)
-    def _():
-        pl.semaphore_signal(barrier, inc=1, device_id={"sx": sx + 1}, device_id_type=MESH)
-
-    k_load.start()
-    e_load.start()
-    n_load.start()
+    pl.semaphore_signal(barrier, inc=1, device_id={"sx": lax.rem(sx + 1, nsx)}, device_id_type=MESH)
 
     unit = iota((m, m), 0) == iota((m, m), 1)
     eye_v[...] = jnp.where(unit, 1.0, 0.0).astype(BF)
@@ -94,7 +88,6 @@
         place = jnp.where(rank < half, rank, rank + short)
         d_v[y] = jnp.where(c > 0.5, place, -1.0 - place)
 
-    pl.semaphore_wait(barrier, 1 + jnp.where(sy > 0, 1, 0) + jnp.where(sx > 0, 1, 0))
 
     def to_north(src, dst, send, recv):
         return pltpu.make_async_remote_copy(
@@ -102,44 +95,26 @@
 
     def to_east(src, dst, send, recv):
         return pltpu.make_async_remote_copy(
-            src_ref=src, dst_ref=dst, send_sem=send, recv_sem=recv, device_id={"sx": sx - 1}, device_id_type=MESH)
-
-    dn_copy = to_north(d_v.at[0], dn_out, ds_sem.at[0], dr_sem.at[0])
-    de_copy = to_east(d_v.at[:, 0:8], de_out, ds_sem.at[1], dr_sem.at[1])
-    zn_copies = [to_north(zns_v.at[x], zn_out.at[x], zs_sem.at[x], zr_sem.at[x]) for x in range(xs)]
+            src_ref=src, dst_ref=dst, send_sem=send, recv_sem=recv, device_id={"sx": lax.rem(sx + nsx - 1, nsx)}, device_id_type=MESH)
+
+    dn_copy = to_north(d_v.at[0], dnr_v, ds_sem.at[0], dr_sem.at[0])
+    de_copy = to_east(d_v.at[:, 0:8], der_v, ds_sem.at[1], dr_sem.at[1])
+    zn_copies = [to_north(zns_v.at[a:b], zn_out.at[a:b], zs_sem.at[k], zr_sem.at[k]) for k, (a, b) in enumerate(groups)]
     ze_copies = [
         to_east(zns_v.at[0] if y == 0 else zes_v.at[y], ze_out.at[y], es_sem.at[y], er_sem.at[y]) for y in range(ys)
     ]
     p_copies = [
         pltpu.make_async_remote_copy(
-            src_ref=p_v.at[y], dst_ref=other_out.at[y], send_sem=ps_sem.at[y], recv_sem=pr_sem.at[y],
+            src_ref=p_v.at[y], dst_ref=other_v.at[y], send_sem=ps_sem.at[y], recv_sem=pr_sem.at[y],
             device_id=partner, device_id_type=MESH)
         for y in range(ys)
     ]
 
-    @pl.when(sy > 0)
-    def _():
-        dn_copy.start()
-
-    @pl.when(sx > 0)
-    def _():
-        de_copy.start()
-
     @pl.when(sy == nsy - 1)
     def _():
-        dn_out[...] = jnp.full(dn_out.shape, -1.0, F32)
+        dnr_v[...] = jnp.zeros(dnr_v.shape, F32)
         zn_out[...] = jnp.zeros(zn_out.shape, BF)
 
-    @pl.when(sx == nsx - 1)
-    def _():
-        de_out[...] = jnp.full(de_out.shape, -1.0, F32)
-        ze_out[...] = jnp.zeros(ze_out.shape, BF)
-
-    shift_load.wait()
-    for t, (x, f) in enumerate(tiles):
-        row = s_v[f, x]
-        for y in range(ys):
-            s_r[y, t : t + 1, :] = row[y : y + 1, :]
 
     def interpolate(y):
         for x in range(xs):
@@ -180,32 +155,51 @@
             parts.append(x_v[y, t, :half, :half] + turned[:half, half:] + turned[half:, :half])
         return jnp.concatenate(parts, axis=1)
 
+    prompt = sy != nsy // 2
     w_loads[0].wait()
+    shift_load.start()
+    for copy in w_loads[1:]:
+        copy.start()
+    k_load.start()
+    e_load.start()
+    n_load.start()
+    shift_load.wait()
+    for t, (x, f) in enumerate(tiles):
+        row = s_v[f, x]
+        for y in range(ys):
+            s_r[y, t : t + 1, :] = row[y : y + 1, :]
     interpolate(0)
-    squeeze(0, tiles)
-    for x in range(xs):
-        zns_v[x] = folded(0, x)
-
-        @pl.when(sy > 0)
+    for k, (a, b) in enumerate(groups):
+        squeeze(0, tiles[a * fields : b * fields])
+        for x in range(a, b):
+            zns_v[x] = folded(0, x)
+
+        if k == 0:
+            @pl.when(prompt)
+            def _():
+                pl.semaphore_wait(barrier, jnp.where(sy > 0, 3, 2))
+
+        @pl.when(prompt & (sy > 0))
         def _():
-            zn_copies[x].start()
-
-    @pl.when(sx > 0)
-    def _():
-        ze_copies[0].start()
-
-    p_copies[0].start()
+            if k == 0:
+                dn_copy.start()
+            zn_copies[k].start()
+
+    @pl.when(prompt)
+    def _():
+        for copy in [de_copy, ze_copies[0], p_copies[0]]:
+            copy.start()
+
     for y in range(1, ys):
         w_loads[y].wait()
         interpolate(y)
         squeeze(y, tiles[:fields])
         zes_v[y] = folded(y, 0)
 
-        @pl.when(sx > 0)
-        def _():
-            ze_copies[y].start()
-
-        p_copies[y].start()
+    @pl.when(prompt)
+    def _():
+        for copy in ze_copies[1:] + p_copies[1:]:
+            copy.start()
 
     for y in range(ys):
         for x, f in tiles:
@@ -220,13 +214,19 @@
                 k_r[y, j * PAD + t : j * PAD + t + 1, :] = row[y : y + 1, :]
     for y in range(ys):
         k_r[y, :PAD, :] = k_r[y, :PAD, :] + a_r[y]
-        kt_out[y] = k_r[y].T
+        kt_v[y] = k_r[y].T
+
+    @pl.when(jnp.logical_not(prompt))
+    def _():
+        pl.semaphore_wait(barrier, 3)
+        for copy in [dn_copy, de_copy] + zn_copies + ze_copies + p_copies:
+            copy.start()
 
     e_load.wait()
     n_load.wait()
 
     def column(j, y, t):
-        return kt_out[y, :, j * PAD + t : j * PAD + t + 1]
+        return kt_v[y, :, j * PAD + t : j * PAD + t + 1]
 
     for y in range(ys):
         for t, (x, f) in enumerate(tiles):
@@ -253,38 +253,38 @@
     def _():
         dn_copy.wait_recv()
 
-    @pl.when(sx < nsx - 1)
-    def _():
-        de_copy.wait_recv()
-
-    def reorder(tile, dest):
-        return mm(tile, jnp.concatenate([fine_hot(dest, m), coarse_hot(dest, m)], axis=0), NT).astype(BF)
-
-    for t, (x, f) in enumerate(tiles):
-        ne_out[t] = reorder(n_v[f, x, ys - 1], dn_out[t : t + 1, :])
+    de_copy.wait()
+    dn_out[...] = jnp.where(sy < nsy - 1, dnr_v[...], m * 4.0)
+    de_out[...] = jnp.where(sx < nsx - 1, der_v[...], m * 4.0)
+
+    def reorder(r, tile, dest):
+        ne_out[r] = mm(tile, jnp.concatenate([fine_hot(dest, m), coarse_hot(dest, m)], axis=0), NT).astype(BF)
+
+    for t, (x, f) in enumerate(tiles):
+        reorder(t, n_v[f, x, ys - 1], dn_out[t : t + 1, :])
     for y in range(ys):
         for f in range(fields):
-            ne_out[len(tiles) + y * fields + f] = reorder(e_v[f, xs - 1, y], de_out[y, f : f + 1, :])
-
-    @pl.when(sy > 0)
-    def _():
-        dn_copy.wait_send()
-        for copy in zn_copies:
-            copy.wait_send()
-
-    @pl.when(sx > 0)
-    def _():
-        de_copy.wait_send()
-        for copy in ze_copies:
-            copy.wait_send()
+            reorder(len(tiles) + y * fields + f, e_v[f, xs - 1, y], de_out[y, f : f + 1, :])
 
     for copy in p_copies:
         copy.wait()
-
-    @pl.when(sx < nsx - 1)
-    def _():
-        for copy in ze_copies:
-            copy.wait_recv()
+    for y in range(ys):
+        for t, (x, f) in enumerate(tiles):
+            for g in range(fields):
+                wo_v[y, x, f, :, g * m : (g + 1) * m] = (column(2 + g, y, t) * other_v[y, x, g].astype(F32)).astype(BF)
+    for y in range(ys):
+        for x, f in tiles:
+            res = mm(q_out[y, x, f], wo_v[y, x, f])
+            for g in range(fields):
+                cross_out[f, g, x, y] = res[:, g * m : (g + 1) * m].astype(BF)
+
+    for copy in ze_copies:
+        copy.wait()
+
+    @pl.when(sy > 0)
+    def _():
+        for copy in [dn_copy] + zn_copies:
+            copy.wait_send()
 
     @pl.when(sy < nsy - 1)
     def _():
@@ -293,9 +293,9 @@
 
 
 def finish_kernel(
-    dims, q, other, node_own, east_in, north_in, zn, ze, dn, de, ne, kt,
+    dims, q, cross, node_own, east_in, north_in, zn, ze, dn, de, ne,
     node_out, east_out, north_out,
-    wt_v, node_v, full_v, im_v, pk_v, nrim_v, erim_v, own_sem, int_sem, cross_sem, rim_sem,
+    full_v, im_v, pk_v, nrim_v, erim_v, own_sem, int_sem, cross_sem, rim_sem,
 ):
     fields, xs, ys, m = dims
     half = m // 2
@@ -312,25 +312,10 @@
     for f in range(fields):
         for g in range(fields):
             put(node_own.at[f, g], node_out.at[f, own0 + g], own_sem.at[f, g])
+            put(cross.at[f, g], node_out.at[f, oth0 + g], cross_sem.at[f, g])
     for f in range(fields):
         put(east_in.at[f, : xs - 1], east_out.at[f, : xs - 1], int_sem.at[0, f])
         put(north_in.at[f, :, 0], north_out.at[f, :, 0], int_sem.at[1, f])
-
-    def column(j, y, t):
-        return kt[y, :, j * PAD + t : j * PAD + t + 1]
-
-    for y in range(ys):
-        for t, (x, f) in enumerate(tiles):
-            for g in range(fields):
-                wt_v[y, x, f, :, g * m : (g + 1) * m] = (column(2 + g, y, t) * other[y, x, g].astype(F32)).astype(BF)
-    for x in range(xs):
-        for f in range(fields):
-            for y in range(ys):
-                res = mm(q[y, x, f], wt_v[y, x, f])
-                for g in range(fields):
-                    node_v[f, g, x, y] = res[:, g * m : (g + 1) * m].astype(BF)
-            for g in range(fields):
-                put(node_v.at[f, g, x], node_out.at[f, oth0 + g, x], cross_sem.at[f, g, x])
 
     rims = []
     for t, (x, f) in enumerate(tiles):
@@ -384,7 +369,7 @@
             exchange,
             out_shape=[
                 pltpu.VMEM((ys, xs, fields, m, m), BF),
-                pltpu.VMEM((ys, xs, fields, m, m), BF),
+                pltpu.VMEM((fields, fields, xs, ys, m, m), BF),
                 pltpu.VMEM((fields, fields, xs, ys, m, m), BF),
                 pltpu.VMEM((fields, xs, ys, m, m), BF),
                 pltpu.VMEM((fields, xs, ys, m, m), BF),
@@ -393,10 +378,9 @@
                 pltpu.VMEM((PAD, m), F32),
                 pltpu.VMEM((ys, 8, m), F32),
                 pltpu.VMEM((rims, m, 2 * m), BF),
-                pltpu.VMEM((ys, m, m), F32),
             ],
             in_specs=[hbm] * 6,
-            out_specs=[vmem] * 11,
+            out_specs=[vmem] * 10,
             scratch_shapes=[
                 pltpu.VMEM((ys, fields, xs, m, m), BF),
                 pltpu.VMEM((fields, xs, ys, m, m), BF),
@@ -421,8 +405,13 @@
                 pltpu.VMEM((ys, half, m), BF),
                 pltpu.VMEM((m, m), BF),
                 pltpu.VMEM((m, m), BF),
+                pltpu.VMEM((PAD, m), F32),
+                pltpu.VMEM((ys, 8, m), F32),
+                pltpu.VMEM((ys, xs, fields, m, m), BF),
+                pltpu.VMEM((ys, xs, fields, m, 2 * m), BF),
+                pltpu.VMEM((ys, m, m), F32),
                 dma((ys,)), dma((3,)), dma((2,)),
-                dma((xs,)), dma((xs,)), dma((ys,)), dma((ys,)), dma((2,)), dma((2,)), dma((ys,)), dma((ys,)),
+                dma((2,)), dma((2,)), dma((ys,)), dma((ys,)), dma((2,)), dma((2,)), dma((ys,)), dma((ys,)),
             ],
             compiler_params=pltpu.CompilerParams(
                 collective_id=0, has_side_effects=True, vmem_limit_bytes=32 * MIB
@@ -440,17 +429,15 @@
                 jax.ShapeDtypeStruct((fields, xs, ys, m, m), BF),
                 jax.ShapeDtypeStruct((fields, xs, ys, m, m), BF),
             ],
-            in_specs=[vmem] * 11,
+            in_specs=[vmem] * 10,
             out_specs=[hbm] * 3,
             scratch_shapes=[
-                pltpu.VMEM((ys, xs, fields, m, 2 * m), BF),
-                pltpu.VMEM((fields, fields, xs, ys, m, m), BF),
                 pltpu.VMEM((rims, m, m), BF),
                 pltpu.VMEM((rims, m, m), BF),
                 pltpu.VMEM((rims, m, m), BF),
                 pltpu.VMEM((fields, xs, m, m), BF),
                 pltpu.VMEM((fields, ys, m, m), BF),
-                dma((fields, fields)), dma((2, fields)), dma((fields, fields, xs)), dma((2, fields)),
+                dma((fields, fields)), dma((2, fields)), dma((fields, fields)), dma((2, fields)),
             ],
             compiler_params=pltpu.CompilerParams(vmem_limit_bytes=24 * MIB),
             name="finish",

time: 21.4 us -> 17.8 us (0.83)
  the two profiles are of different devices: /device:TPU:22 before, /device:TPU:1 now
where the time goes in v3:
time: 17.8 us; the launch traced here: 17.7 us
  Pallas kernels  17.1 us (96%)
  between operations  0.64 us (4%)
    pallas_call x1, Pallas kernels, body(): pl.pallas_call(exchange, out_shape=[pltpu.VMEM((ys, xs, fields, m, m), BF...  12.9 us
    pallas_call x1, Pallas kernels, body(): pl.pallas_call(finish, out_shape=[jax.ShapeDtypeStruct((fields, every, xs...  4.15 us

profile of v3, /device:TPU:1, one launch (start us, length us, event | category | flops | bytes accessed | tf_op | source)
XLA Modules:
  0.0 17.7 jit_solution(8223757695442499885)
XLA Ops:
  0.6 12.9 %exchange.1 = (bf16[2,10,2,128,128]{4,3,2,1,0:T(8,128)(2,1)S(1)}, bf16[2,2,10,2,128,128]{5,4,3,2,1,0:T(8,128)(2,1)S(1)}, bf16[2,2,10,2,128,128]{5,4,3,2,1,0:T(8,...) custom-call(bf16[2,10,2,128,128]{4,3,2,1,0:T(8,128)(2,1)} %refs_0_.1, ...), custom_call_target="tpu_custom_call" | custom-call | tf_op jit(solution)/shard_map/exchange/pallas_call | solution.py:368
  13.6 4.2 %finish.1 = (bf16[2,4,10,2,128,128]{5,4,3,2,1,0:T(8,128)(2,1)}, bf16[2,10,2,128,128]{4,3,2,1,0:T(8,128)(2,1)}, bf16[2,10,2,128,128]{4,3,2,1,0:T(8,128)(2,1)}) custom-call(bf16[2,10,2,128,128]{4,3,2,1,0:T(8,128)(2,1)S(1)} %get-tuple-element.13.refs_0_, bf16[2,2,10,2,128,128]{5,4,3,2,1,0:T(8,128)(2,1)S(1)} %get-tuple-element.14.refs_1_, ...), custom_call_target="tpu_custom_call" | custom-call | tf_op jit(solution)/shard_map/finish/pallas_call | solution.py:425

commit v4 on v3

--- a/solution.py
+++ b/solution.py
@@ -32,9 +32,9 @@
 
 def exchange_kernel(
     dims, inner, east, north, shift, coupling, flags,
-    q_out, cross_out, node_out, east_out, north_out, zn_out, ze_out, dn_out, de_out, ne_out,
+    q_out, other_out, node_out, east_out, north_out, zn_out, ze_out, dn_out, de_out, ne_out, kt_out,
     w_v, e_v, n_v, s_v, k_v, c_v, p_v, w0_v, wt_v, c_r, s_r, a_r, tot_r, str_r, k_r, fac_t, d_v, y_v, x_v,
-    zns_v, zes_v, eye_v, off_v, dnr_v, der_v, other_v, wo_v, kt_v,
+    zns_v, zes_v, eye_v, off_v, dnr_v, der_v,
     w_sem, vec_sem, en_sem, zs_sem, zr_sem, es_sem, er_sem, ds_sem, dr_sem, ps_sem, pr_sem,
 ):
     nsx, nsy, fields, xs, ys, m = dims
@@ -53,6 +53,7 @@
     e_load = pltpu.make_async_copy(east, e_v, en_sem.at[0])
     n_load = pltpu.make_async_copy(north, n_v, en_sem.at[1])
     flag_load.start()
+    shift_load.start()
     w_loads[0].start()
 
     pl.semaphore_signal(barrier, inc=1, device_id=partner, device_id_type=MESH)
@@ -105,7 +106,7 @@
     ]
     p_copies = [
         pltpu.make_async_remote_copy(
-            src_ref=p_v.at[y], dst_ref=other_v.at[y], send_sem=ps_sem.at[y], recv_sem=pr_sem.at[y],
+            src_ref=p_v.at[y], dst_ref=other_out.at[y], send_sem=ps_sem.at[y], recv_sem=pr_sem.at[y],
             device_id=partner, device_id_type=MESH)
         for y in range(ys)
     ]
@@ -156,18 +157,17 @@
         return jnp.concatenate(parts, axis=1)
 
     prompt = sy != nsy // 2
+    shift_load.wait()
+    for t, (x, f) in enumerate(tiles):
+        row = s_v[f, x]
+        for y in range(ys):
+            s_r[y, t : t + 1, :] = row[y : y + 1, :]
     w_loads[0].wait()
-    shift_load.start()
     for copy in w_loads[1:]:
         copy.start()
     k_load.start()
     e_load.start()
     n_load.start()
-    shift_load.wait()
-    for t, (x, f) in enumerate(tiles):
-        row = s_v[f, x]
-        for y in range(ys):
-            s_r[y, t : t + 1, :] = row[y : y + 1, :]
     interpolate(0)
     for k, (a, b) in enumerate(groups):
         squeeze(0, tiles[a * fields : b * fields])
@@ -214,7 +214,7 @@
                 k_r[y, j * PAD + t : j * PAD + t + 1, :] = row[y : y + 1, :]
     for y in range(ys):
         k_r[y, :PAD, :] = k_r[y, :PAD, :] + a_r[y]
-        kt_v[y] = k_r[y].T
+        kt_out[y] = k_r[y].T
 
     @pl.when(jnp.logical_not(prompt))
     def _():
@@ -226,7 +226,7 @@
     n_load.wait()
 
     def column(j, y, t):
-        return kt_v[y, :, j * PAD + t : j * PAD + t + 1]
+        return kt_out[y, :, j * PAD + t : j * PAD + t + 1]
 
     for y in range(ys):
         for t, (x, f) in enumerate(tiles):
@@ -268,15 +268,6 @@
 
     for copy in p_copies:
         copy.wait()
-    for y in range(ys):
-        for t, (x, f) in enumerate(tiles):
-            for g in range(fields):
-                wo_v[y, x, f, :, g * m : (g + 1) * m] = (column(2 + g, y, t) * other_v[y, x, g].astype(F32)).astype(BF)
-    for y in range(ys):
-        for x, f in tiles:
-            res = mm(q_out[y, x, f], wo_v[y, x, f])
-            for g in range(fields):
-                cross_out[f, g, x, y] = res[:, g * m : (g + 1) * m].astype(BF)
 
     for copy in ze_copies:
         copy.wait()
@@ -293,9 +284,9 @@
 
 
 def finish_kernel(
-    dims, q, cross, node_own, east_in, north_in, zn, ze, dn, de, ne,
+    dims, q, other, node_own, east_in, north_in, zn, ze, dn, de, ne, kt,
     node_out, east_out, north_out,
-    full_v, im_v, pk_v, nrim_v, erim_v, own_sem, int_sem, cross_sem, rim_sem,
+    wt_v, node_v, full_v, im_v, pk_v, nrim_v, erim_v, own_sem, int_sem, cross_sem, rim_sem,
 ):
     fields, xs, ys, m = dims
     half = m // 2
@@ -312,10 +303,25 @@
     for f in range(fields):
         for g in range(fields):
             put(node_own.at[f, g], node_out.at[f, own0 + g], own_sem.at[f, g])
-            put(cross.at[f, g], node_out.at[f, oth0 + g], cross_sem.at[f, g])
     for f in range(fields):
         put(east_in.at[f, : xs - 1], east_out.at[f, : xs - 1], int_sem.at[0, f])
         put(north_in.at[f, :, 0], north_out.at[f, :, 0], int_sem.at[1, f])
+
+    def column(j, y, t):
+        return kt[y, :, j * PAD + t : j * PAD + t + 1]
+
+    for y in range(ys):
+        for t, (x, f) in enumerate(tiles):
+            for g in range(fields):
+                wt_v[y, x, f, :, g * m : (g + 1) * m] = (column(2 + g, y, t) * other[y, x, g].astype(F32)).astype(BF)
+    for x in range(xs):
+        for f in range(fields):
+            for y in range(ys):
+                res = mm(q[y, x, f], wt_v[y, x, f])
+                for g in range(fields):
+                    node_v[f, g, x, y] = res[:, g * m : (g + 1) * m].astype(BF)
+            for g in range(fields):
+                put(node_v.at[f, g, x], node_out.at[f, oth0 + g, x], cross_sem.at[f, g, x])
 
     rims = []
     for t, (x, f) in enumerate(tiles):
@@ -333,16 +339,17 @@
         im_v[r] = (mm(ne[r, :, :m], full_v[r]) + ne[r, :, m:].astype(F32)).astype(BF)
     for r, (_, _, _, tile, _) in enumerate(rims):
         pk_v[r] = (-mm(tile[...], im_v[r])).astype(BF)
-    for t, (x, f) in enumerate(tiles):
-        nrim_v[f, x] = mm(pk_v[t], coarse_hot(rims[t][4][...], m)).astype(BF)
-    for f in range(fields):
-        put(nrim_v.at[f], north_out.at[f, :, ys - 1], rim_sem.at[0, f])
     for y in range(ys):
         for f in range(fields):
             r = len(tiles) + y * fields + f
             erim_v[f, y] = mm(pk_v[r], coarse_hot(rims[r][4][...], m)).astype(BF)
     for f in range(fields):
         put(erim_v.at[f], east_out.at[f, xs - 1], rim_sem.at[1, f])
+    for f in range(fields):
+        for x in range(xs):
+            t = x * fields + f
+            nrim_v[f, x] = mm(pk_v[t], coarse_hot(rims[t][4][...], m)).astype(BF)
+        put(nrim_v.at[f], north_out.at[f, :, ys - 1], rim_sem.at[0, f])
     for copy in copies:
         copy.wait()
 
@@ -369,7 +376,7 @@
             exchange,
             out_shape=[
                 pltpu.VMEM((ys, xs, fields, m, m), BF),
-                pltpu.VMEM((fields, fields, xs, ys, m, m), BF),
+                pltpu.VMEM((ys, xs, fields, m, m), BF),
                 pltpu.VMEM((fields, fields, xs, ys, m, m), BF),
                 pltpu.VMEM((fields, xs, ys, m, m), BF),
                 pltpu.VMEM((fields, xs, ys, m, m), BF),
@@ -378,9 +385,10 @@
                 pltpu.VMEM((PAD, m), F32),
                 pltpu.VMEM((ys, 8, m), F32),
                 pltpu.VMEM((rims, m, 2 * m), BF),
+                pltpu.VMEM((ys, m, m), F32),
             ],
             in_specs=[hbm] * 6,
-            out_specs=[vmem] * 10,
+            out_specs=[vmem] * 11,
             scratch_shapes=[
                 pltpu.VMEM((ys, fields, xs, m, m), BF),
                 pltpu.VMEM((fields, xs, ys, m, m), BF),
@@ -407,9 +415,6 @@
                 pltpu.VMEM((m, m), BF),
                 pltpu.VMEM((PAD, m), F32),
                 pltpu.VMEM((ys, 8, m), F32),
-                pltpu.VMEM((ys, xs, fields, m, m), BF),
-                pltpu.VMEM((ys, xs, fields, m, 2 * m), BF),
-                pltpu.VMEM((ys, m, m), F32),
                 dma((ys,)), dma((3,)), dma((2,)),
                 dma((2,)), dma((2,)), dma((ys,)), dma((ys,)), dma((2,)), dma((2,)), dma((ys,)), dma((ys,)),
             ],
@@ -429,15 +434,17 @@
                 jax.ShapeDtypeStruct((fields, xs, ys, m, m), BF),
                 jax.ShapeDtypeStruct((fields, xs, ys, m, m), BF),
             ],
-            in_specs=[vmem] * 10,
+            in_specs=[vmem] * 11,
             out_specs=[hbm] * 3,
             scratch_shapes=[
+                pltpu.VMEM((ys, xs, fields, m, 2 * m), BF),
+                pltpu.VMEM((fields, fields, xs, ys, m, m), BF),
                 pltpu.VMEM((rims, m, m), BF),
                 pltpu.VMEM((rims, m, m), BF),
                 pltpu.VMEM((rims, m, m), BF),
                 pltpu.VMEM((fields, xs, m, m), BF),
                 pltpu.VMEM((fields, ys, m, m), BF),
-                dma((fields, fields)), dma((2, fields)), dma((fields, fields)), dma((2, fields)),
+                dma((fields, fields)), dma((2, fields)), dma((fields, fields, xs)), dma((2, fields)),
             ],
             compiler_params=pltpu.CompilerParams(vmem_limit_bytes=24 * MIB),
             name="finish",

time: 17.8 us -> 17.2 us (0.966)
  the two profiles are of different devices: /device:TPU:1 before, /device:TPU:96 now
where the time goes in v4:
time: 17.2 us; the launch traced here: 17.1 us
  Pallas kernels  16.5 us (96%)
  between operations  0.64 us (4%)
    pallas_call x1, Pallas kernels, body(): pl.pallas_call(exchange, out_shape=[pltpu.VMEM((ys, xs, fields, m, m), BF...  11.6 us
    pallas_call x1, Pallas kernels, body(): pl.pallas_call(finish, out_shape=[jax.ShapeDtypeStruct((fields, every, xs...  4.85 us

profile of v4, /device:TPU:96, one launch (start us, length us, event | category | flops | bytes accessed | tf_op | source)
XLA Modules:
  0.0 17.1 jit_solution(5641149258206035132)
XLA Ops:
  0.6 11.6 %exchange.1 = (bf16[2,10,2,128,128]{4,3,2,1,0:T(8,128)(2,1)S(1)}, bf16[2,10,2,128,128]{4,3,2,1,0:T(8,128)(2,1)S(1)}, bf16[2,2,10,2,128,128]{5,4,3,2,1,0:T(8,128)...) custom-call(bf16[2,10,2,128,128]{4,3,2,1,0:T(8,128)(2,1)} %refs_0_.1, ...), custom_call_target="tpu_custom_call" | custom-call | tf_op jit(solution)/shard_map/exchange/pallas_call | solution.py:375
  12.3 4.8 %finish.1 = (bf16[2,4,10,2,128,128]{5,4,3,2,1,0:T(8,128)(2,1)}, bf16[2,10,2,128,128]{4,3,2,1,0:T(8,128)(2,1)}, bf16[2,10,2,128,128]{4,3,2,1,0:T(8,128)(2,1)}) custom-call(bf16[2,10,2,128,128]{4,3,2,1,0:T(8,128)(2,1)S(1)} %get-tuple-element.14.refs_0_, bf16[2,10,2,128,128]{4,3,2,1,0:T(8,128)(2,1)S(1)} %get-tuple-element.15.refs_1_, ...), custom_call_target="tpu_custom_call" | custom-call | tf_op jit(solution)/shard_map/finish/pallas_call | solution.py:430

commit v5 on v4

--- a/solution.py
+++ b/solution.py
@@ -314,15 +314,6 @@
         for t, (x, f) in enumerate(tiles):
             for g in range(fields):
                 wt_v[y, x, f, :, g * m : (g + 1) * m] = (column(2 + g, y, t) * other[y, x, g].astype(F32)).astype(BF)
-    for x in range(xs):
-        for f in range(fields):
-            for y in range(ys):
-                res = mm(q[y, x, f], wt_v[y, x, f])
-                for g in range(fields):
-                    node_v[f, g, x, y] = res[:, g * m : (g + 1) * m].astype(BF)
-            for g in range(fields):
-                put(node_v.at[f, g, x], node_out.at[f, oth0 + g, x], cross_sem.at[f, g, x])
-
     rims = []
     for t, (x, f) in enumerate(tiles):
         rims.append((zn, x, f, q.at[ys - 1, x, f], dn.at[t : t + 1, :]))
@@ -337,6 +328,15 @@
         full_v[r, half:, half:] = jnp.zeros((half, half), BF)
     for r in range(len(rims)):
         im_v[r] = (mm(ne[r, :, :m], full_v[r]) + ne[r, :, m:].astype(F32)).astype(BF)
+    for x in range(xs):
+        for f in range(fields):
+            for y in range(ys):
+                res = mm(q[y, x, f], wt_v[y, x, f])
+                for g in range(fields):
+                    node_v[f, g, x, y] = res[:, g * m : (g + 1) * m].astype(BF)
+            for g in range(fields):
+                put(node_v.at[f, g, x], node_out.at[f, oth0 + g, x], cross_sem.at[f, g, x])
+
     for r, (_, _, _, tile, _) in enumerate(rims):
         pk_v[r] = (-mm(tile[...], im_v[r])).astype(BF)
     for y in range(ys):

time: 17.2 us -> 17.1 us (level)
  no operation moved by 1% of the time
where the time goes in v5:
time: 17.1 us; the launch traced here: 17 us
  Pallas kernels  16.4 us (96%)
  between operations  0.64 us (4%)
    pallas_call x1, Pallas kernels, body(): pl.pallas_call(exchange, out_shape=[pltpu.VMEM((ys, xs, fields, m, m), BF...  11.6 us
    pallas_call x1, Pallas kernels, body(): pl.pallas_call(finish, out_shape=[jax.ShapeDtypeStruct((fields, every, xs...  4.72 us

profile of v5, /device:TPU:96, one launch (start us, length us, event | category | flops | bytes accessed | tf_op | source)
XLA Modules:
  0.0 17.0 jit_solution(1249617998780502541)
XLA Ops:
  0.6 11.6 %exchange.1 = (bf16[2,10,2,128,128]{4,3,2,1,0:T(8,128)(2,1)S(1)}, bf16[2,10,2,128,128]{4,3,2,1,0:T(8,128)(2,1)S(1)}, bf16[2,2,10,2,128,128]{5,4,3,2,1,0:T(8,128)...) custom-call(bf16[2,10,2,128,128]{4,3,2,1,0:T(8,128)(2,1)} %refs_0_.1, ...), custom_call_target="tpu_custom_call" | custom-call | tf_op jit(solution)/shard_map/exchange/pallas_call | solution.py:375
  12.3 4.7 %finish.1 = (bf16[2,4,10,2,128,128]{5,4,3,2,1,0:T(8,128)(2,1)}, bf16[2,10,2,128,128]{4,3,2,1,0:T(8,128)(2,1)}, bf16[2,10,2,128,128]{4,3,2,1,0:T(8,128)(2,1)}) custom-call(bf16[2,10,2,128,128]{4,3,2,1,0:T(8,128)(2,1)S(1)} %get-tuple-element.14.refs_0_, bf16[2,10,2,128,128]{4,3,2,1,0:T(8,128)(2,1)S(1)} %get-tuple-element.15.refs_1_, ...), custom_call_target="tpu_custom_call" | custom-call | tf_op jit(solution)/shard_map/finish/pallas_call | solution.py:430
